TPU v7x, 512 devices: a whole 4x4x16 slice. The times are simulated.
512 devices in a mesh: orb: 64 (over z, y), st: 8 (over x, core).
Axes of the slice: x: 4, y: 4, z: 16, core: 2. Of those that a mesh axis runs over, the one named last changes fastest.
Arguments:
- wavefunction: float32 [2, 1024, 65536], P(None, 'st', 'orb'), may hold values from -6 to 6
- slope_prev: float32 [2, 1024, 65536], P(None, 'st', 'orb'), may hold values from -6 to 6
- hopping: bfloat16 [1024, 14, 64, 64], P('orb', None, 'st'), may hold values from -0.1875 to 0.1875
- offsets: int32 [1024, 14], P('orb'), may hold values from -16 to 16
- counts: int32 [1024], P('orb'), may hold values from 7 to 14
- bond_vectors: float32 [3, 1024, 14], P(None, 'orb'), may hold values from -6 to 6
- shifts: int32 [3, 1024, 14], P(None, 'orb'), may hold values from -1 to 1
- vector_potential: float32 [3], replicated, may hold values from -1 to 1
Outputs:
- slope_next: float32 [2, 1024, 65536], P(None, 'st', 'orb')
All inputs are finite; a program needn't handle non-finite values.
Results may differ from a plain program's by a relative error of at most 0.0003.
Values may be sent and summed in bfloat16 or wider, within the bound.
No kernel may reach another device: no remote copies, remote signals or barrier semaphores. Data moves between devices by JAX's collectives and lax.ppermute only.
A program may use at most 64 MiB of HBM per device.

v0:
```python
import jax
import jax.numpy as jnp
from jax import lax
from jax.sharding import PartitionSpec as P


def extended_2(x, sides, width):
    for axis, dim in sides:
        size, length = (lax.axis_size(axis), x.shape[dim])
        up = [(i, (i + 1) % size) for i in range(size)]
        down = [(j, i) for i, j in up]
        last = lax.slice_in_dim(x, length - width, length, axis=dim)
        initial = lax.slice_in_dim(x, 0, width, axis=dim)
        before = lax.ppermute(last, axis, up)
        after = lax.ppermute(initial, axis, down)
        x = jnp.concatenate([before, x, after], axis=dim)
    return x


def slot_terms(tiles, source, columns, cosine, sine):
    blocks = tiles.shape[0]
    tile_rows = tiles.shape[2]
    states = source.shape[1]

    def one_slot(slot_index, totals):
        total_re, total_im = totals
        column_now = lax.dynamic_index_in_dim(columns, slot_index, 1, keepdims=False)
        picked = jnp.take(source, column_now, axis=2)
        tile_slab = lax.dynamic_index_in_dim(tiles, slot_index, 1, keepdims=False).astype(
            jnp.float32
        )
        product = jnp.einsum("iab,nsib->nsia", tile_slab, picked, precision=lax.Precision.HIGHEST)
        cos_w = lax.dynamic_index_in_dim(cosine, slot_index, 1, keepdims=False)[None, :, None]
        sin_w = lax.dynamic_index_in_dim(sine, slot_index, 1, keepdims=False)[None, :, None]
        return (
            total_re + cos_w * product[1] + sin_w * product[0],
            total_im + sin_w * product[1] - cos_w * product[0],
        )

    empty = jnp.zeros((states, blocks, tile_rows), jnp.float32)
    total_re, total_im = lax.fori_loop(0, tiles.shape[1], one_slot, (empty, empty))
    return jnp.stack([total_re, total_im])


def summed_terms(tiles, sources):
    result = None
    for source, columns, cosine, sine in sources:
        terms = slot_terms(tiles, source, columns, cosine, sine)
        result = terms
    return result


def on_device(
    wavefunction, slope_prev, hopping, offsets, counts, bond_vectors, shifts, vector_potential
):
    blocks = hopping.shape[0]
    block_width = hopping.shape[3]
    states = wavefunction.shape[1]
    segment = wavefunction + 0.25 * slope_prev
    theta = jnp.zeros(offsets.shape, jnp.float32)
    for axis_index in range(3):
        theta = theta + vector_potential[axis_index] * (
            bond_vectors[axis_index] + 2.0 * shifts[axis_index].astype(jnp.float32)
        )
    live = (jnp.arange(offsets.shape[1], dtype=jnp.int32)[None, :] < counts[:, None]).astype(
        jnp.float32
    )
    cosine = jnp.cos(theta) * live
    sine = jnp.sin(theta) * live
    target = jnp.arange(blocks, dtype=jnp.int32)[:, None] + offsets
    extended_columns = target + blocks
    extended = extended_2(segment, (("orb", 2),), blocks * block_width)
    extended = extended.reshape(2, states, 3 * blocks, block_width)
    sources = [(extended, extended_columns, cosine, sine)]
    tiles = lax.all_gather(hopping, "st", axis=2, tiled=True)
    result = summed_terms(tiles, sources)
    return result.reshape(2, states, blocks * block_width)


def solution(mesh):
    return jax.shard_map(
        on_device,
        mesh=mesh,
        in_specs=(
            P(None, "st", "orb"),
            P(None, "st", "orb"),
            P("orb", None, "st", None),
            P("orb", None),
            P("orb"),
            P(None, "orb", None),
            P(None, "orb", None),
            P(),
        ),
        out_specs=P(None, "st", "orb"),
        check_vma=False,
    )
```

profile of v0, /device:TPU:1, one launch (start us, length us, event | category | flops | bytes accessed | tf_op | source)
XLA Modules:
  0.0 129.3 jit_solution(18306723740621149428)
XLA Ops:
  6.5 2.0 %copy.31 = bf16[16,14,8,64]{3,2,0,1:T(8,128)(2,1)} copy(bf16[16,14,8,64]{3,2,1,0:T(8,128)(2,1)} %param.12) | data formatting | bytes 458752 | tf_op args[2]
  8.6 1.6 %copy.29 = f32[2,128,1024]{1,2,0:T(8,128)S(1)} copy(f32[2,128,1024]{2,1,0:T(8,128)} %param.11) | data formatting | bytes 2097152 | tf_op args[1]
  10.2 0.3 copy.30
  10.5 1.1 multiply_add_fusion
  11.6 4.0 %collective-permute-start = (f32[2,128,1024]{1,2,0:T(8,128)}, f32[2,128,1024]{1,2,0:T(8,128)S(1)}, u32[]{:S(2)}, u32[]{:S(2)}) collective-permute-start(f32[2,128,1024]{1,2,0:T(8,128)} %multiply_add_fusion), channel_id=1, source_target_pairs={{0,8},{8,16},{16,24},{24,32},{32,40},{40,48},{48,56},{56,64},{64,7... | collective-permute-start | bytes 3145736 | tf_op jit(solution)/shard_map/ppermute | solution.py:14
  15.6 12.3 %collective-permute-start.1 = (f32[2,128,1024]{1,2,0:T(8,128)}, f32[2,128,1024]{1,2,0:T(8,128)S(1)}, u32[]{:S(2)}, u32[]{:S(2)}) collective-permute-start(f32[2,128,1024]{1,2,0:T(8,128)} %multiply_add_fusion), channel_id=1, source_target_pairs={{8,0},{16,8},{24,16},{32,24},{40,32},{48,40},{56,48},{64,56},{72,6... | collective-permute-start | bytes 3145736 | tf_op jit(solution)/shard_map/ppermute | solution.py:15
  28.0 0.1 copy.35
  28.1 0.1 copy.36
  28.1 0.1 copy.37
  28.2 0.1 copy.38
  28.3 0.1 copy.39
  28.4 0.1 copy.40
  28.5 0.1 copy.28
  28.6 0.7 fusion.14
  29.2 1.8 %bitcast_select_fusion = (f32[16,14]{0,1:T(8,128)S(1)}, f32[1,16,14]{1,2,0:T(8,128)S(1)}) fusion(s32[16]{0:T(128)S(1)} %copy-done.5, f32[1,16,14]{1,2,0:T(8,128)S(1)} %copy.39, s32[1,16,14]{1,2,0:T(8,128)S(1)} %copy.40, f32[]{:T(128)} %bitcast.2, f32[1,16,14]{1,2,0:T(8,128)S(1)} %copy.37, s32[1,16,14]{1,2,0:T(8,128)S(1)} %copy.38, f32[]{:T(128)} %bitcast.1, ...), kind=kLoop, calls=%fused_computation.27 | loop fusion | flops 3584 | bytes 7244 | tf_op jit(solution)/shard_map/mul | solution.py:69
  31.1 18.0 %collective-permute-done = f32[2,128,1024]{1,2,0:T(8,128)S(1)} collective-permute-done((f32[2,128,1024]{1,2,0:T(8,128)}, f32[2,128,1024]{1,2,0:T(8,128)S(1)}, u32[]{:S(2)}, u32[]{:S(2)}) %collective-permute-start) | collective-permute-done | bytes 1048608 | tf_op jit(solution)/shard_map/ppermute | solution.py:14
  49.1 1.0 collective-permute-done.1
  50.1 3.1 %pad_maximum_fusion = f32[2,128,3072]{1,2,0:T(8,128)} fusion(f32[2,128,1024]{1,2,0:T(8,128)S(1)} %collective-permute-done.1, f32[2,128,1024]{1,2,0:T(8,128)} %multiply_add_fusion, f32[2,128,1024]{1,2,0:T(8,128)S(1)} %collective-permute-done), kind=kLoop, calls=%fused_computation.24 | loop fusion | flops 1572864 | bytes 6291456 | tf_op jit(solution)/shard_map/concatenate | solution.py:16
  53.2 3.6 %all-gather.2.cloned.1.call-done = bf16[16,14,64,64]{3,2,0,1:T(8,128)(2,1)} async-done(((bf16[16,14,8,64]{3,2,0,1:T(8,128)(2,1)}), bf16[16,14,64,64]{3,2,0,1:T(8,128)(2,1)}) %all-gather.2.cloned.1.call-update) | async-done | bytes 1835024 | tf_op jit(solution)/shard_map/all_gather | solution.py:75
  56.7 64.3 %while.16 = (s32[]{:T(128)}, f32[128,16,64]{0,2,1:T(8,128)S(1)}, f32[128,16,64]{0,2,1:T(8,128)S(1)}, f32[16,14]{0,1:T(8,128)S(1)}, s32[16,14]{0,1:T(8,128)S(1)},...) while((s32[]{:T(128)}, f32[128,16,64]{0,2,1:T(8,128)S(1)}, ...), condition=%wide.region_1.2_spmd.clone, body=%wide.region_0.1_spmd.clone.sunk | while | flops 202900576 | bytes 7607575 | solution.py:41
  56.8 2.5 %gather_fusion = f32[16,2,128,64]{2,3,1,0:T(8,128)S(1)} fusion(f32[2,128,48,64]{1,3,2,0:T(8,128)} %get-tuple-element.293, s32[1024]{0:T(1024)S(1)} %pad_clamp_fusion.2), kind=kCustom, calls=%fused_computation.clone.clone.1 | custom fusion | bytes 2097216 | tf_op jit(solution)/shard_map/while/body/eval_jaxpr/jit(_take)/gather | solution.py:28
  59.3 1.7 %convolution_bitcast_fusion.2 = f32[2,128,16,64]{1,3,0,2:T(8,128)S(1)} fusion(f32[16,2,128,64]{2,3,1,0:T(8,128)S(1)} %gather_fusion, pred[16]{0:T(512)(128)(4,1)S(1)} %get-tuple-element.263, bf16[16,14,64,64]{3,2,0,1:T(8,128)(2,1)} %get-tuple-element.294, s32[]{:T(128)} %get-tuple-element.278), kind=kOutput, calls=%fused_computation.1.clone.1 | convolution fusion | flops 201588736 | bytes 2359824 | tf_op jit(solution)/shard_map/while/body/eval_jaxpr/iab,nsib->nsia/dot_general | solution.py:32
  61.0 0.3 fusion.22
  61.4 2.5 %gather_fusion = f32[16,2,128,64]{2,3,1,0:T(8,128)S(1)} fusion(f32[2,128,48,64]{1,3,2,0:T(8,128)} %get-tuple-element.293, s32[1024]{0:T(1024)S(1)} %pad_clamp_fusion.2), kind=kCustom, calls=%fused_computation.clone.clone.1 | custom fusion | bytes 2097216 | tf_op jit(solution)/shard_map/while/body/eval_jaxpr/jit(_take)/gather | solution.py:28
  63.9 1.7 %convolution_bitcast_fusion.2 = f32[2,128,16,64]{1,3,0,2:T(8,128)S(1)} fusion(f32[16,2,128,64]{2,3,1,0:T(8,128)S(1)} %gather_fusion, pred[16]{0:T(512)(128)(4,1)S(1)} %get-tuple-element.263, bf16[16,14,64,64]{3,2,0,1:T(8,128)(2,1)} %get-tuple-element.294, s32[]{:T(128)} %get-tuple-element.278), kind=kOutput, calls=%fused_computation.1.clone.1 | convolution fusion | flops 201588736 | bytes 2359824 | tf_op jit(solution)/shard_map/while/body/eval_jaxpr/iab,nsib->nsia/dot_general | solution.py:32
  65.6 0.3 fusion.22
  66.0 2.5 %gather_fusion = f32[16,2,128,64]{2,3,1,0:T(8,128)S(1)} fusion(f32[2,128,48,64]{1,3,2,0:T(8,128)} %get-tuple-element.293, s32[1024]{0:T(1024)S(1)} %pad_clamp_fusion.2), kind=kCustom, calls=%fused_computation.clone.clone.1 | custom fusion | bytes 2097216 | tf_op jit(solution)/shard_map/while/body/eval_jaxpr/jit(_take)/gather | solution.py:28
  68.5 1.7 %convolution_bitcast_fusion.2 = f32[2,128,16,64]{1,3,0,2:T(8,128)S(1)} fusion(f32[16,2,128,64]{2,3,1,0:T(8,128)S(1)} %gather_fusion, pred[16]{0:T(512)(128)(4,1)S(1)} %get-tuple-element.263, bf16[16,14,64,64]{3,2,0,1:T(8,128)(2,1)} %get-tuple-element.294, s32[]{:T(128)} %get-tuple-element.278), kind=kOutput, calls=%fused_computation.1.clone.1 | convolution fusion | flops 201588736 | bytes 2359824 | tf_op jit(solution)/shard_map/while/body/eval_jaxpr/iab,nsib->nsia/dot_general | solution.py:32
  70.2 0.3 fusion.22
  70.6 2.5 %gather_fusion = f32[16,2,128,64]{2,3,1,0:T(8,128)S(1)} fusion(f32[2,128,48,64]{1,3,2,0:T(8,128)} %get-tuple-element.293, s32[1024]{0:T(1024)S(1)} %pad_clamp_fusion.2), kind=kCustom, calls=%fused_computation.clone.clone.1 | custom fusion | bytes 2097216 | tf_op jit(solution)/shard_map/while/body/eval_jaxpr/jit(_take)/gather | solution.py:28
  73.1 1.7 %convolution_bitcast_fusion.2 = f32[2,128,16,64]{1,3,0,2:T(8,128)S(1)} fusion(f32[16,2,128,64]{2,3,1,0:T(8,128)S(1)} %gather_fusion, pred[16]{0:T(512)(128)(4,1)S(1)} %get-tuple-element.263, bf16[16,14,64,64]{3,2,0,1:T(8,128)(2,1)} %get-tuple-element.294, s32[]{:T(128)} %get-tuple-element.278), kind=kOutput, calls=%fused_computation.1.clone.1 | convolution fusion | flops 201588736 | bytes 2359824 | tf_op jit(solution)/shard_map/while/body/eval_jaxpr/iab,nsib->nsia/dot_general | solution.py:32
  74.8 0.3 fusion.22
  75.2 2.5 %gather_fusion = f32[16,2,128,64]{2,3,1,0:T(8,128)S(1)} fusion(f32[2,128,48,64]{1,3,2,0:T(8,128)} %get-tuple-element.293, s32[1024]{0:T(1024)S(1)} %pad_clamp_fusion.2), kind=kCustom, calls=%fused_computation.clone.clone.1 | custom fusion | bytes 2097216 | tf_op jit(solution)/shard_map/while/body/eval_jaxpr/jit(_take)/gather | solution.py:28
  77.7 1.7 %convolution_bitcast_fusion.2 = f32[2,128,16,64]{1,3,0,2:T(8,128)S(1)} fusion(f32[16,2,128,64]{2,3,1,0:T(8,128)S(1)} %gather_fusion, pred[16]{0:T(512)(128)(4,1)S(1)} %get-tuple-element.263, bf16[16,14,64,64]{3,2,0,1:T(8,128)(2,1)} %get-tuple-element.294, s32[]{:T(128)} %get-tuple-element.278), kind=kOutput, calls=%fused_computation.1.clone.1 | convolution fusion | flops 201588736 | bytes 2359824 | tf_op jit(solution)/shard_map/while/body/eval_jaxpr/iab,nsib->nsia/dot_general | solution.py:32
  79.4 0.3 fusion.22
  79.8 2.5 %gather_fusion = f32[16,2,128,64]{2,3,1,0:T(8,128)S(1)} fusion(f32[2,128,48,64]{1,3,2,0:T(8,128)} %get-tuple-element.293, s32[1024]{0:T(1024)S(1)} %pad_clamp_fusion.2), kind=kCustom, calls=%fused_computation.clone.clone.1 | custom fusion | bytes 2097216 | tf_op jit(solution)/shard_map/while/body/eval_jaxpr/jit(_take)/gather | solution.py:28
  82.3 1.7 %convolution_bitcast_fusion.2 = f32[2,128,16,64]{1,3,0,2:T(8,128)S(1)} fusion(f32[16,2,128,64]{2,3,1,0:T(8,128)S(1)} %gather_fusion, pred[16]{0:T(512)(128)(4,1)S(1)} %get-tuple-element.263, bf16[16,14,64,64]{3,2,0,1:T(8,128)(2,1)} %get-tuple-element.294, s32[]{:T(128)} %get-tuple-element.278), kind=kOutput, calls=%fused_computation.1.clone.1 | convolution fusion | flops 201588736 | bytes 2359824 | tf_op jit(solution)/shard_map/while/body/eval_jaxpr/iab,nsib->nsia/dot_general | solution.py:32
  84.0 0.3 fusion.22
  84.3 2.5 %gather_fusion = f32[16,2,128,64]{2,3,1,0:T(8,128)S(1)} fusion(f32[2,128,48,64]{1,3,2,0:T(8,128)} %get-tuple-element.293, s32[1024]{0:T(1024)S(1)} %pad_clamp_fusion.2), kind=kCustom, calls=%fused_computation.clone.clone.1 | custom fusion | bytes 2097216 | tf_op jit(solution)/shard_map/while/body/eval_jaxpr/jit(_take)/gather | solution.py:28
  86.9 1.7 %convolution_bitcast_fusion.2 = f32[2,128,16,64]{1,3,0,2:T(8,128)S(1)} fusion(f32[16,2,128,64]{2,3,1,0:T(8,128)S(1)} %gather_fusion, pred[16]{0:T(512)(128)(4,1)S(1)} %get-tuple-element.263, bf16[16,14,64,64]{3,2,0,1:T(8,128)(2,1)} %get-tuple-element.294, s32[]{:T(128)} %get-tuple-element.278), kind=kOutput, calls=%fused_computation.1.clone.1 | convolution fusion | flops 201588736 | bytes 2359824 | tf_op jit(solution)/shard_map/while/body/eval_jaxpr/iab,nsib->nsia/dot_general | solution.py:32
  88.6 0.3 fusion.22
  88.9 2.5 %gather_fusion = f32[16,2,128,64]{2,3,1,0:T(8,128)S(1)} fusion(f32[2,128,48,64]{1,3,2,0:T(8,128)} %get-tuple-element.293, s32[1024]{0:T(1024)S(1)} %pad_clamp_fusion.2), kind=kCustom, calls=%fused_computation.clone.clone.1 | custom fusion | bytes 2097216 | tf_op jit(solution)/shard_map/while/body/eval_jaxpr/jit(_take)/gather | solution.py:28
  91.5 1.7 %convolution_bitcast_fusion.2 = f32[2,128,16,64]{1,3,0,2:T(8,128)S(1)} fusion(f32[16,2,128,64]{2,3,1,0:T(8,128)S(1)} %gather_fusion, pred[16]{0:T(512)(128)(4,1)S(1)} %get-tuple-element.263, bf16[16,14,64,64]{3,2,0,1:T(8,128)(2,1)} %get-tuple-element.294, s32[]{:T(128)} %get-tuple-element.278), kind=kOutput, calls=%fused_computation.1.clone.1 | convolution fusion | flops 201588736 | bytes 2359824 | tf_op jit(solution)/shard_map/while/body/eval_jaxpr/iab,nsib->nsia/dot_general | solution.py:32
  93.2 0.3 fusion.22
  93.5 2.5 %gather_fusion = f32[16,2,128,64]{2,3,1,0:T(8,128)S(1)} fusion(f32[2,128,48,64]{1,3,2,0:T(8,128)} %get-tuple-element.293, s32[1024]{0:T(1024)S(1)} %pad_clamp_fusion.2), kind=kCustom, calls=%fused_computation.clone.clone.1 | custom fusion | bytes 2097216 | tf_op jit(solution)/shard_map/while/body/eval_jaxpr/jit(_take)/gather | solution.py:28
  96.1 1.7 %convolution_bitcast_fusion.2 = f32[2,128,16,64]{1,3,0,2:T(8,128)S(1)} fusion(f32[16,2,128,64]{2,3,1,0:T(8,128)S(1)} %gather_fusion, pred[16]{0:T(512)(128)(4,1)S(1)} %get-tuple-element.263, bf16[16,14,64,64]{3,2,0,1:T(8,128)(2,1)} %get-tuple-element.294, s32[]{:T(128)} %get-tuple-element.278), kind=kOutput, calls=%fused_computation.1.clone.1 | convolution fusion | flops 201588736 | bytes 2359824 | tf_op jit(solution)/shard_map/while/body/eval_jaxpr/iab,nsib->nsia/dot_general | solution.py:32
  97.8 0.3 fusion.22
  98.1 2.5 %gather_fusion = f32[16,2,128,64]{2,3,1,0:T(8,128)S(1)} fusion(f32[2,128,48,64]{1,3,2,0:T(8,128)} %get-tuple-element.293, s32[1024]{0:T(1024)S(1)} %pad_clamp_fusion.2), kind=kCustom, calls=%fused_computation.clone.clone.1 | custom fusion | bytes 2097216 | tf_op jit(solution)/shard_map/while/body/eval_jaxpr/jit(_take)/gather | solution.py:28
  100.7 1.7 %convolution_bitcast_fusion.2 = f32[2,128,16,64]{1,3,0,2:T(8,128)S(1)} fusion(f32[16,2,128,64]{2,3,1,0:T(8,128)S(1)} %gather_fusion, pred[16]{0:T(512)(128)(4,1)S(1)} %get-tuple-element.263, bf16[16,14,64,64]{3,2,0,1:T(8,128)(2,1)} %get-tuple-element.294, s32[]{:T(128)} %get-tuple-element.278), kind=kOutput, calls=%fused_computation.1.clone.1 | convolution fusion | flops 201588736 | bytes 2359824 | tf_op jit(solution)/shard_map/while/body/eval_jaxpr/iab,nsib->nsia/dot_general | solution.py:32
  102.4 0.3 fusion.22
  102.7 2.5 %gather_fusion = f32[16,2,128,64]{2,3,1,0:T(8,128)S(1)} fusion(f32[2,128,48,64]{1,3,2,0:T(8,128)} %get-tuple-element.293, s32[1024]{0:T(1024)S(1)} %pad_clamp_fusion.2), kind=kCustom, calls=%fused_computation.clone.clone.1 | custom fusion | bytes 2097216 | tf_op jit(solution)/shard_map/while/body/eval_jaxpr/jit(_take)/gather | solution.py:28
  105.3 1.7 %convolution_bitcast_fusion.2 = f32[2,128,16,64]{1,3,0,2:T(8,128)S(1)} fusion(f32[16,2,128,64]{2,3,1,0:T(8,128)S(1)} %gather_fusion, pred[16]{0:T(512)(128)(4,1)S(1)} %get-tuple-element.263, bf16[16,14,64,64]{3,2,0,1:T(8,128)(2,1)} %get-tuple-element.294, s32[]{:T(128)} %get-tuple-element.278), kind=kOutput, calls=%fused_computation.1.clone.1 | convolution fusion | flops 201588736 | bytes 2359824 | tf_op jit(solution)/shard_map/while/body/eval_jaxpr/iab,nsib->nsia/dot_general | solution.py:32
  107.0 0.3 fusion.22
  107.3 2.5 %gather_fusion = f32[16,2,128,64]{2,3,1,0:T(8,128)S(1)} fusion(f32[2,128,48,64]{1,3,2,0:T(8,128)} %get-tuple-element.293, s32[1024]{0:T(1024)S(1)} %pad_clamp_fusion.2), kind=kCustom, calls=%fused_computation.clone.clone.1 | custom fusion | bytes 2097216 | tf_op jit(solution)/shard_map/while/body/eval_jaxpr/jit(_take)/gather | solution.py:28
  109.8 1.7 %convolution_bitcast_fusion.2 = f32[2,128,16,64]{1,3,0,2:T(8,128)S(1)} fusion(f32[16,2,128,64]{2,3,1,0:T(8,128)S(1)} %gather_fusion, pred[16]{0:T(512)(128)(4,1)S(1)} %get-tuple-element.263, bf16[16,14,64,64]{3,2,0,1:T(8,128)(2,1)} %get-tuple-element.294, s32[]{:T(128)} %get-tuple-element.278), kind=kOutput, calls=%fused_computation.1.clone.1 | convolution fusion | flops 201588736 | bytes 2359824 | tf_op jit(solution)/shard_map/while/body/eval_jaxpr/iab,nsib->nsia/dot_general | solution.py:32
  111.6 0.3 fusion.22
  111.9 2.5 %gather_fusion = f32[16,2,128,64]{2,3,1,0:T(8,128)S(1)} fusion(f32[2,128,48,64]{1,3,2,0:T(8,128)} %get-tuple-element.293, s32[1024]{0:T(1024)S(1)} %pad_clamp_fusion.2), kind=kCustom, calls=%fused_computation.clone.clone.1 | custom fusion | bytes 2097216 | tf_op jit(solution)/shard_map/while/body/eval_jaxpr/jit(_take)/gather | solution.py:28
  114.4 1.7 %convolution_bitcast_fusion.2 = f32[2,128,16,64]{1,3,0,2:T(8,128)S(1)} fusion(f32[16,2,128,64]{2,3,1,0:T(8,128)S(1)} %gather_fusion, pred[16]{0:T(512)(128)(4,1)S(1)} %get-tuple-element.263, bf16[16,14,64,64]{3,2,0,1:T(8,128)(2,1)} %get-tuple-element.294, s32[]{:T(128)} %get-tuple-element.278), kind=kOutput, calls=%fused_computation.1.clone.1 | convolution fusion | flops 201588736 | bytes 2359824 | tf_op jit(solution)/shard_map/while/body/eval_jaxpr/iab,nsib->nsia/dot_general | solution.py:32
  116.2 0.3 fusion.22
  116.5 2.5 %gather_fusion = f32[16,2,128,64]{2,3,1,0:T(8,128)S(1)} fusion(f32[2,128,48,64]{1,3,2,0:T(8,128)} %get-tuple-element.293, s32[1024]{0:T(1024)S(1)} %pad_clamp_fusion.2), kind=kCustom, calls=%fused_computation.clone.clone.1 | custom fusion | bytes 2097216 | tf_op jit(solution)/shard_map/while/body/eval_jaxpr/jit(_take)/gather | solution.py:28
  119.0 1.7 %convolution_bitcast_fusion.2 = f32[2,128,16,64]{1,3,0,2:T(8,128)S(1)} fusion(f32[16,2,128,64]{2,3,1,0:T(8,128)S(1)} %gather_fusion, pred[16]{0:T(512)(128)(4,1)S(1)} %get-tuple-element.263, bf16[16,14,64,64]{3,2,0,1:T(8,128)(2,1)} %get-tuple-element.294, s32[]{:T(128)} %get-tuple-element.278), kind=kOutput, calls=%fused_computation.1.clone.1 | convolution fusion | flops 201588736 | bytes 2359824 | tf_op jit(solution)/shard_map/while/body/eval_jaxpr/iab,nsib->nsia/dot_general | solution.py:32
  120.8 0.3 fusion.22
  121.1 0.1 pad_maximum_fusion.1
  121.2 1.3 %copy.32 = f32[2,128,1024]{2,1,0:T(8,128)} copy(f32[2,128,1024]{1,2,0:T(8,128)S(1)} %pad_maximum_fusion.1) | data formatting | bytes 2097152 | tf_op jit(solution)/shard_map/stack | solution.py:42
  (62 shorter events, 0.6 us)
Async XLA Ops:
  6.5 3.6 %copy-start = (f32[2,128,1024]{2,1,0:T(8,128)S(1)}, f32[2,128,1024]{2,1,0:T(8,128)}, u32[]{:S(2)}) copy-start(f32[2,128,1024]{2,1,0:T(8,128)} %param.10) | copy-start | bytes 3145732
  6.5 50.2 %all-gather.2.cloned.1.call-start = ((), (), s32[]{:S(2)}) async-start(), calls=%async_computation | async-start | bytes 4128768 | tf_op jit(solution)/shard_map/all_gather | solution.py:75
  8.6 19.4 %copy-start.1 = (f32[3,16,14]{2,1,0:T(8,128)S(1)}, f32[3,16,14]{2,1,0:T(8,128)}, u32[]{:S(2)}) copy-start(f32[3,16,14]{2,1,0:T(8,128)} %param.15) | copy-start | bytes 8068
  10.1 17.9 %copy-start.2 = (s32[3,16,14]{2,1,0:T(8,128)S(1)}, s32[3,16,14]{2,1,0:T(8,128)}, u32[]{:S(2)}) copy-start(s32[3,16,14]{2,1,0:T(8,128)} %param.16) | copy-start | bytes 8068
  10.2 18.3 %copy-start.3 = (s32[16,14]{1,0:T(8,128)S(1)}, s32[16,14]{1,0:T(8,128)}, u32[]{:S(2)}) copy-start(s32[16,14]{1,0:T(8,128)} %param.13) | copy-start | bytes 2692
  10.2 18.4 %copy-start.4 = (f32[3]{0:T(128)S(1)}, f32[3]{0:T(128)}, u32[]{:S(2)}) copy-start(f32[3]{0:T(128)} %param.17) | copy-start | bytes 40
  10.2 19.0 %copy-start.5 = (s32[16]{0:T(128)S(1)}, s32[16]{0:T(128)}, u32[]{:S(2)}) copy-start(s32[16]{0:T(128)} %param.14) | copy-start | bytes 196
  11.6 37.5 %collective-permute-start = (f32[2,128,1024]{1,2,0:T(8,128)}, f32[2,128,1024]{1,2,0:T(8,128)S(1)}, u32[]{:S(2)}, u32[]{:S(2)}) collective-permute-start(f32[2,128,1024]{1,2,0:T(8,128)} %multiply_add_fusion), channel_id=1, source_target_pairs={{0,8},{8,16},{16,24},{24,32},{32,40},{40,48},{48,56},{56,64},{64,7... | collective-permute-start | bytes 3145736 | tf_op jit(solution)/shard_map/ppermute | solution.py:14
  15.6 34.4 %collective-permute-start.1 = (f32[2,128,1024]{1,2,0:T(8,128)}, f32[2,128,1024]{1,2,0:T(8,128)S(1)}, u32[]{:S(2)}, u32[]{:S(2)}) collective-permute-start(f32[2,128,1024]{1,2,0:T(8,128)} %multiply_add_fusion), channel_id=1, source_target_pairs={{8,0},{16,8},{24,16},{32,24},{40,32},{48,40},{56,48},{64,56},{72,6... | collective-permute-start | bytes 3145736 | tf_op jit(solution)/shard_map/ppermute | solution.py:15
Sparse Core Ops, SparseCore 0:
  9.5 47.2 all-gather.1
where the time goes:
time: 131 us; the launch traced here: 129 us
  local copies, waits for them, and re-layouts  41.7 us (32%)
  matrix products  24.3 us (19%)
  waiting for transfers between devices  22.5 us (17%)
  starting transfers between devices  16.3 us (12%)
  between operations  13.5 us (10%)
  other arithmetic  10.2 us (8%)
    gather x14, local copies, waits for them, and re-layouts, one_slot(): picked = jnp.take(source, column_now, axis=2)  35 us
    dot_general x14, matrix products, one_slot(): jnp.einsum('iab,nsib->nsia', tile_slab, picked, precision=lax.Precision.H...  24.3 us
    ppermute x1, waiting for transfers between devices, extended_2(): before = lax.ppermute(last, axis, up)  18 us
    ppermute x1, starting transfers between devices, extended_2(): after = lax.ppermute(initial, axis, down)  12.3 us
    unnamed x22, local copies, waits for them, and re-layouts  4.48 us
    ppermute x1, starting transfers between devices, extended_2(): before = lax.ppermute(last, axis, up)  4.02 us
    sub x14, other arithmetic, one_slot(): total_im + sin_w * product[1] - cos_w * product[0]  3.74 us
    all_gather x1, waiting for transfers between devices, on_device(): tiles = lax.all_gather(hopping, 'st', axis=2, tiled=True)  3.58 us
  transfers between devices with their start and end apart: 3, of which 3 were waited for; matrix products, arithmetic and copies ran while one was open for 7% of the time, Pallas kernels for 0%

commit v1 on v0

v1 whole, which is shorter than its diff:
```python
import functools

import jax
import jax.numpy as jnp
from jax import lax
from jax.experimental import pallas as pl
from jax.experimental.pallas import tpu as pltpu
from jax.sharding import PartitionSpec as P

VMEM = pltpu.VMEM
SMEM = pltpu.SMEM
F32 = jnp.float32
BF16 = jnp.bfloat16
LEVELS = 32767.0
STEPS = 256.0
TINY = 1e-37


def split(x):
    hi = x.astype(BF16)
    return hi, (x - hi.astype(F32)).astype(BF16)


def tiles_kernel(hop_ref, off_ref, cnt_ref, bond_ref, shift_ref, vp_ref, hop_out, cos_out, sin_out, col_out):
    blocks, slots, rows, width = hop_ref.shape
    for i in range(blocks):
        hop_out[i] = jnp.concatenate([hop_ref[i, s] for s in range(slots)], axis=1)
    theta = jnp.zeros(off_ref.shape, F32)
    for k in range(3):
        theta = theta + vp_ref[k] * (bond_ref[k] + 2.0 * shift_ref[k].astype(F32))
    live = lax.broadcasted_iota(jnp.int32, theta.shape, 1) < cnt_ref[...]
    cos_out[...] = jnp.where(live, jnp.cos(theta), 0.0)
    sin_out[...] = jnp.where(live, jnp.sin(theta), 0.0)
    row = lax.broadcasted_iota(jnp.int32, theta.shape, 0)
    col_out[...] = off_ref[...] + row + blocks


def segment_kernel(width, wave_ref, slope_ref, own_ref, pay_ref):
    states = wave_ref.shape[1]
    blocks = wave_ref.shape[2] // width
    codes = []
    for c in range(blocks * width // 128):
        cols = pl.ds(c * 128, 128)
        seg = wave_ref[:, :, cols] + 0.25 * slope_ref[:, :, cols]
        both = jnp.concatenate([seg[0].T, seg[1].T], axis=1)
        hi, lo = split(both)
        for k in range(128 // width):
            j = c * (128 // width) + k
            part = both[k * width : (k + 1) * width]
            own_ref[j, 0:width] = hi[k * width : (k + 1) * width]
            own_ref[j, width : 2 * width] = lo[k * width : (k + 1) * width]
            top = jnp.maximum(jnp.max(jnp.abs(part), axis=0, keepdims=True), TINY)
            code = jnp.ceil(jnp.log2(top) * STEPS) + 1.0
            codes.append(code)
            q = jnp.round(part * (LEVELS * jnp.exp2(code * (-1.0 / STEPS))))
            pay_ref[j * width : (j + 1) * width] = q.astype(jnp.int32).astype(jnp.int16)
    pay_ref[blocks * width :] = jnp.concatenate(codes, axis=0).astype(jnp.int32).astype(jnp.int16)


def slots_kernel(hop_ref, own_ref, prev_ref, next_ref, cos_ref, sin_ref, col_ref, out_ref, xs):
    blocks, rows, depth = hop_ref.shape
    slots = cos_ref.shape[1]
    width = depth // slots
    states = out_ref.shape[1]

    def own(j, _):
        xs[blocks + j] = own_ref[j]
        return 0

    lax.fori_loop(0, blocks, own, 0, unroll=4)
    for base, ref in ((0, prev_ref), (2 * blocks, next_ref)):
        code = ref[blocks * width :].astype(jnp.int32).astype(F32)
        scale = jnp.exp2(code * (1.0 / STEPS)) * (1.0 / LEVELS)
        for j in range(blocks):
            q = ref[j * width : (j + 1) * width].astype(jnp.int32).astype(F32)
            hi, lo = split(q * scale[j : j + 1])
            xs[base + j, 0:width] = hi
            xs[base + j, width : 2 * width] = lo

    def block_pair(pair, _):
        res = []
        for k in range(2):
            i = 2 * pair + k
            a = jnp.zeros((rows, 2 * states), F32)
            b = jnp.zeros((rows, 2 * states), F32)
            for p in range(slots // 2):
                tile = hop_ref[i, :, 2 * width * p : 2 * width * (p + 1)]
                for h in range(2):
                    s = 2 * p + h
                    half = tile[:, h * width : (h + 1) * width]
                    prod = jnp.dot(
                        jnp.concatenate([half, half], axis=1), xs[col_ref[i, s]], preferred_element_type=F32
                    )
                    a = a + cos_ref[i, s] * prod
                    b = b + sin_ref[i, s] * prod
            res.append((a[:, states:] + b[:, :states], b[:, states:] - a[:, :states]))
        cols = pl.ds(pl.multiple_of(pair * 2 * rows, 2 * rows), 2 * rows)
        out_ref[0, :, cols] = jnp.concatenate([res[0][0], res[1][0]], axis=0).T
        out_ref[1, :, cols] = jnp.concatenate([res[0][1], res[1][1]], axis=0).T
        return 0

    lax.fori_loop(0, blocks // 2, block_pair, 0)


def on_device(
    wavefunction, slope_prev, hopping, offsets, counts, bond_vectors, shifts, vector_potential
):
    blocks, slots, rows, width = hopping.shape
    states = wavefunction.shape[1]
    orbs = blocks * width
    table = jax.ShapeDtypeStruct((blocks, slots), F32)
    vm = pl.BlockSpec(memory_space=VMEM)
    sm = pl.BlockSpec(memory_space=SMEM)
    params = pltpu.CompilerParams(vmem_limit_bytes=40 * 1024 * 1024)
    part, cosine, sine, columns = pl.pallas_call(
        tiles_kernel,
        out_shape=(
            jax.ShapeDtypeStruct((blocks, rows, slots * width), BF16),
            table,
            table,
            jax.ShapeDtypeStruct((blocks, slots), jnp.int32),
        ),
        in_specs=[vm] * 5 + [sm],
        out_specs=[vm] * 4,
        compiler_params=params,
        name="tiles",
    )(hopping, offsets, counts[:, None], bond_vectors, shifts, vector_potential)
    tiles = lax.all_gather(part, "st", axis=1, tiled=True)
    own, payload = pl.pallas_call(
        functools.partial(segment_kernel, width),
        out_shape=(
            jax.ShapeDtypeStruct((blocks, 2 * width, 2 * states), BF16),
            jax.ShapeDtypeStruct((orbs + blocks, 2 * states), jnp.int16),
        ),
        in_specs=[vm] * 2,
        out_specs=[vm] * 2,
        compiler_params=params,
        name="segment",
    )(wavefunction, slope_prev)
    size = lax.axis_size("orb")
    up = [(i, (i + 1) % size) for i in range(size)]
    down = [(j, i) for i, j in up]
    before = lax.ppermute(payload, "orb", up)
    after = lax.ppermute(payload, "orb", down)
    return pl.pallas_call(
        slots_kernel,
        out_shape=jax.ShapeDtypeStruct((2, states, orbs), F32),
        in_specs=[vm] * 4 + [sm] * 3,
        out_specs=vm,
        scratch_shapes=[VMEM((3 * blocks, 2 * width, 2 * states), BF16)],
        compiler_params=params,
        name="slots",
    )(tiles, own, before, after, cosine, sine, columns)


def solution(mesh):
    return jax.shard_map(
        on_device,
        mesh=mesh,
        in_specs=(
            P(None, "st", "orb"),
            P(None, "st", "orb"),
            P("orb", None, "st", None),
            P("orb", None),
            P("orb"),
            P(None, "orb", None),
            P(None, "orb", None),
            P(),
        ),
        out_specs=P(None, "st", "orb"),
        check_vma=False,
    )
```

time: 131 us -> 66.8 us (0.51)
  local copies, waits for them, and re-layouts: 41.7 us -> 8.52 us
  matrix products: 24.3 us -> 0 us
  other arithmetic: 10.2 us -> 0 us
  Pallas kernels: 0 us -> 8.63 us
  waiting for transfers between devices: 22.5 us -> 19.4 us
    gather x14 -> x0, local copies, waits for them, and re-layouts: 35 us -> none  [one_slot(): picked = jnp.take(source, column_now, axis=2)]
    dot_general x14 -> x0, matrix products: 24.3 us -> none  [one_slot(): jnp.einsum('iab,nsib->nsia', tile_slab, picked, precision=lax.Precision.H...]
    pallas_call x0 -> x3, Pallas kernels: none -> 8.63 us  [the longest x1 6.79 us: on_device(): pl.pallas_call(slots_kernel, out_shape=jax.ShapeDtypeStruct((2, states, o...]
    sub x14 -> x0, other arithmetic: 3.74 us -> none  [one_slot(): total_im + sin_w * product[1] - cos_w * product[0]]
    unnamed x22 -> x16, local copies, waits for them, and re-layouts: 4.48 us -> 7.79 us
    concatenate x1 -> x0, other arithmetic: 3.1 us -> none  [extended_2(): x = jnp.concatenate([before, x, after], axis=dim)]
    ppermute x2, waiting for transfers between devices: 18.9 us -> 15.9 us  [the longest x1 8.82 us: on_device(): after = lax.ppermute(payload, 'orb', down)]
    mul x2 -> x0, other arithmetic: 1.89 us -> none  [the longest x1 1.84 us: on_device(): sine = jnp.sin(theta) * live]
  transfers between devices with their start and end apart: 3 -> 3, of which waited for: 3 -> 3; matrix products, arithmetic and copies ran while one was open for 7% -> 0% of each run, Pallas kernels for 0% -> 1%
where the time goes in v1:
time: 66.8 us; the launch traced here: 66.3 us
  waiting for transfers between devices  19.4 us (29%)
  starting transfers between devices  16.3 us (24%)
  between operations  13.4 us (20%)
  Pallas kernels  8.63 us (13%)
  local copies, waits for them, and re-layouts  8.52 us (13%)
    ppermute x1, starting transfers between devices, on_device(): after = lax.ppermute(payload, 'orb', down)  14.4 us
    ppermute x1, waiting for transfers between devices, on_device(): after = lax.ppermute(payload, 'orb', down)  8.82 us
    unnamed x16, local copies, waits for them, and re-layouts  7.79 us
    ppermute x1, waiting for transfers between devices, on_device(): before = lax.ppermute(payload, 'orb', up)  7.12 us
    pallas_call x1, Pallas kernels, on_device(): pl.pallas_call(slots_kernel, out_shape=jax.ShapeDtypeStruct((2, states, o...  6.79 us
    all_gather x1, waiting for transfers between devices, on_device(): tiles = lax.all_gather(part, 'st', axis=1, tiled=True)  3.43 us
    ppermute x1, starting transfers between devices, on_device(): before = lax.ppermute(payload, 'orb', up)  1.92 us
    pallas_call x1, Pallas kernels, on_device(): pl.pallas_call(tiles_kernel, out_shape=(jax.ShapeDtypeStruct((blocks, row...  1.41 us
  transfers between devices with their start and end apart: 3, of which 3 were waited for; matrix products, arithmetic and copies ran while one was open for 0% of the time, Pallas kernels for 1%

profile of v1, /device:TPU:1, one launch (start us, length us, event | category | flops | bytes accessed | tf_op | source)
XLA Modules:
  0.0 66.3 jit_solution(5075196470578222848)
XLA Ops:
  6.5 0.0 all-gather.2.cloned.1.call-start
  6.5 0.7 %copy.9.cnt_ref = s32[16,1]{1,0:T(8,128)S(1)} copy(s32[16,1]{0,1:T(1,128)} %bitcast.1) | data formatting | bytes 128 | tf_op jit(solution)/shard_map/broadcast_in_dim | solution.py:127
  7.3 0.0 copy-start.3
  7.3 1.0 %copy-done.3 = bf16[16,14,8,64]{3,2,1,0:T(8,128)(2,1)S(1)} copy-done((bf16[16,14,8,64]{3,2,1,0:T(8,128)(2,1)S(1)}, bf16[16,14,8,64]{3,2,1,0:T(8,128)(2,1)}, u32[]{:S(2)}) %copy-start.3) | copy-done | bytes 229400
  8.3 0.0 copy-start.4
  8.3 0.7 %copy-done.4 = f32[3,16,14]{2,1,0:T(8,128)S(1)} copy-done((f32[3,16,14]{2,1,0:T(8,128)S(1)}, f32[3,16,14]{2,1,0:T(8,128)}, u32[]{:S(2)}) %copy-start.4) | copy-done | bytes 2712
  9.0 0.0 copy-start.5
  9.0 0.7 %copy-done.5 = s32[3,16,14]{2,1,0:T(8,128)S(1)} copy-done((s32[3,16,14]{2,1,0:T(8,128)S(1)}, s32[3,16,14]{2,1,0:T(8,128)}, u32[]{:S(2)}) %copy-start.5) | copy-done | bytes 2712
  9.8 0.0 copy-start.6
  9.8 0.7 %copy-done.6 = s32[16,14]{1,0:T(8,128)S(1)} copy-done((s32[16,14]{1,0:T(8,128)S(1)}, s32[16,14]{1,0:T(8,128)}, u32[]{:S(2)}) %copy-start.6) | copy-done | bytes 920
  10.5 0.0 copy-start.7
  10.5 0.7 copy-done.7
  11.1 1.4 %tiles.1 = (bf16[16,8,896]{2,1,0:T(8,128)(2,1)}, f32[16,14]{1,0:T(8,128)S(1)}, f32[16,14]{1,0:T(8,128)S(1)}, s32[16,14]{1,0:T(8,128)S(1)}) custom-call(bf16[16,14,8,64]{3,2,1,0:T(8,128)(2,1)S(1)} %copy-done.3, s32[16,14]{1,0:T(8,128)S(1)} %copy-done.6, s32[16,1]{1,0:T(8,128)S(1)} %copy.9.cnt_ref, f32[3,16,14]{2,1,0:T(8,128)S(1)} %copy-done.4, ...), custom_call_target="tpu_custom_call" | custom-call | tf_op jit(solution)/shard_map/tiles/pallas_call | solution.py:115
  12.5 0.0 all-gather.2.cloned.1.call-update
  12.6 0.0 copy-start.1
  12.6 1.2 %copy-done.1 = f32[2,128,1024]{2,1,0:T(8,128)S(1)} copy-done((f32[2,128,1024]{2,1,0:T(8,128)S(1)}, f32[2,128,1024]{2,1,0:T(8,128)}, u32[]{:S(2)}) %copy-start.1) | copy-done | bytes 1048600
  13.8 0.0 copy-start.2
  13.8 1.2 %copy-done.2 = f32[2,128,1024]{2,1,0:T(8,128)S(1)} copy-done((f32[2,128,1024]{2,1,0:T(8,128)S(1)}, f32[2,128,1024]{2,1,0:T(8,128)}, u32[]{:S(2)}) %copy-start.2) | copy-done | bytes 1048600
  15.0 0.4 segment.1
  15.4 14.4 %collective-permute-start.1 = (s16[1040,256]{1,0:T(8,128)(2,1)S(1)}, s16[1040,256]{1,0:T(8,128)(2,1)S(1)}, u32[]{:S(2)}, u32[]{:S(2)}) collective-permute-start(s16[1040,256]{1,0:T(8,128)(2,1)S(1)} %get-tuple-element.13), channel_id=1, source_target_pairs={{8,0},{16,8},{24,16},{32,24},{40,32},{48,40},{56,48},{64,56},{72,6... | collective-permute-start | bytes 1597448 | tf_op jit(solution)/shard_map/ppermute | solution.py:144
  29.9 1.9 %collective-permute-start = (s16[1040,256]{1,0:T(8,128)(2,1)S(1)}, s16[1040,256]{1,0:T(8,128)(2,1)S(1)}, u32[]{:S(2)}, u32[]{:S(2)}) collective-permute-start(s16[1040,256]{1,0:T(8,128)(2,1)S(1)} %get-tuple-element.13), channel_id=1, source_target_pairs={{0,8},{8,16},{16,24},{24,32},{32,40},{40,48},{48,56},{56,64},{64,7... | collective-permute-start | bytes 1597448 | tf_op jit(solution)/shard_map/ppermute | solution.py:143
  31.8 8.8 %collective-permute-done.1.next_ref = s16[1040,256]{1,0:T(8,128)(2,1)S(1)} collective-permute-done((s16[1040,256]{1,0:T(8,128)(2,1)S(1)}, s16[1040,256]{1,0:T(8,128)(2,1)S(1)}, u32[]{:S(2)}, u32[]{:S(2)}) %collective-permute-start.1) | collective-permute-done | bytes 532512 | tf_op jit(solution)/shard_map/ppermute | solution.py:144
  40.6 7.1 %collective-permute-done.prev_ref = s16[1040,256]{1,0:T(8,128)(2,1)S(1)} collective-permute-done((s16[1040,256]{1,0:T(8,128)(2,1)S(1)}, s16[1040,256]{1,0:T(8,128)(2,1)S(1)}, u32[]{:S(2)}, u32[]{:S(2)}) %collective-permute-start) | collective-permute-done | bytes 532512 | tf_op jit(solution)/shard_map/ppermute | solution.py:143
  47.7 3.4 %all-gather.2.cloned.1.call-done.hop_ref = bf16[16,64,896]{2,1,0:T(8,128)(2,1)} async-done(((bf16[16,8,896]{2,1,0:T(8,128)(2,1)}), bf16[16,64,896]{2,1,0:T(8,128)(2,1)}) %all-gather.2.cloned.1.call-update) | async-done | bytes 1835024 | tf_op jit(solution)/shard_map/all_gather | solution.py:128
  51.2 0.0 copy-start
  51.2 1.5 %copy-done = bf16[16,64,896]{2,1,0:T(8,128)(2,1)S(1)} copy-done((bf16[16,64,896]{2,1,0:T(8,128)(2,1)S(1)}, bf16[16,64,896]{2,1,0:T(8,128)(2,1)}, u32[]{:S(2)}) %copy-start) | copy-done | bytes 1835032
  52.7 6.8 %slots.1 = f32[2,128,1024]{2,1,0:T(8,128)} custom-call(bf16[16,64,896]{2,1,0:T(8,128)(2,1)S(1)} %copy-done, bf16[16,128,256]{2,1,0:T(8,128)(2,1)S(1)} %get-tuple-element.12.own_ref, s16[1040,256]{1,0:T(8,128)(2,1)S(1)} %collective-permute-done.prev_ref, s16[1040,256]{1,0:T(8,128)(2,1)S(1)} %collective-permute-done.1.next_ref, ...), custom_call_target="tpu_custom_call" | custom-call | tf_op jit(solution)/shard_map/slots/pallas_call | solution.py:145
Async XLA Ops:
  6.5 44.6 %all-gather.2.cloned.1.call-start = ((), (), s32[]{:S(2)}) async-start(), calls=%async_computation | async-start | bytes 2064384 | tf_op jit(solution)/shard_map/all_gather | solution.py:128
  7.3 1.0 %copy-start.3 = (bf16[16,14,8,64]{3,2,1,0:T(8,128)(2,1)S(1)}, bf16[16,14,8,64]{3,2,1,0:T(8,128)(2,1)}, u32[]{:S(2)}) copy-start(bf16[16,14,8,64]{3,2,1,0:T(8,128)(2,1)} %hop_ref.1) | copy-start | bytes 688132
  8.3 0.7 %copy-start.4 = (f32[3,16,14]{2,1,0:T(8,128)S(1)}, f32[3,16,14]{2,1,0:T(8,128)}, u32[]{:S(2)}) copy-start(f32[3,16,14]{2,1,0:T(8,128)} %bond_ref.1) | copy-start | bytes 8068
  9.0 0.7 %copy-start.5 = (s32[3,16,14]{2,1,0:T(8,128)S(1)}, s32[3,16,14]{2,1,0:T(8,128)}, u32[]{:S(2)}) copy-start(s32[3,16,14]{2,1,0:T(8,128)} %shift_ref.1) | copy-start | bytes 8068
  9.8 0.7 %copy-start.6 = (s32[16,14]{1,0:T(8,128)S(1)}, s32[16,14]{1,0:T(8,128)}, u32[]{:S(2)}) copy-start(s32[16,14]{1,0:T(8,128)} %off_ref.1) | copy-start | bytes 2692
  10.5 0.7 copy-start.7
  12.6 1.2 %copy-start.1 = (f32[2,128,1024]{2,1,0:T(8,128)S(1)}, f32[2,128,1024]{2,1,0:T(8,128)}, u32[]{:S(2)}) copy-start(f32[2,128,1024]{2,1,0:T(8,128)} %wave_ref.1) | copy-start | bytes 3145732
  13.8 1.2 %copy-start.2 = (f32[2,128,1024]{2,1,0:T(8,128)S(1)}, f32[2,128,1024]{2,1,0:T(8,128)}, u32[]{:S(2)}) copy-start(f32[2,128,1024]{2,1,0:T(8,128)} %slope_ref.1) | copy-start | bytes 3145732
  15.4 25.2 %collective-permute-start.1 = (s16[1040,256]{1,0:T(8,128)(2,1)S(1)}, s16[1040,256]{1,0:T(8,128)(2,1)S(1)}, u32[]{:S(2)}, u32[]{:S(2)}) collective-permute-start(s16[1040,256]{1,0:T(8,128)(2,1)S(1)} %get-tuple-element.13), channel_id=1, source_target_pairs={{8,0},{16,8},{24,16},{32,24},{40,32},{48,40},{56,48},{64,56},{72,6... | collective-permute-start | bytes 1597448 | tf_op jit(solution)/shard_map/ppermute | solution.py:144
  29.9 17.9 %collective-permute-start = (s16[1040,256]{1,0:T(8,128)(2,1)S(1)}, s16[1040,256]{1,0:T(8,128)(2,1)S(1)}, u32[]{:S(2)}, u32[]{:S(2)}) collective-permute-start(s16[1040,256]{1,0:T(8,128)(2,1)S(1)} %get-tuple-element.13), channel_id=1, source_target_pairs={{0,8},{8,16},{16,24},{24,32},{32,40},{40,48},{48,56},{56,64},{64,7... | collective-permute-start | bytes 1597448 | tf_op jit(solution)/shard_map/ppermute | solution.py:143
  51.2 1.5 %copy-start = (bf16[16,64,896]{2,1,0:T(8,128)(2,1)S(1)}, bf16[16,64,896]{2,1,0:T(8,128)(2,1)}, u32[]{:S(2)}) copy-start(bf16[16,64,896]{2,1,0:T(8,128)(2,1)} %all-gather.2.cloned.1.call-done.hop_ref) | copy-start | bytes 5505028
Sparse Core Ops, SparseCore 0:
  12.7 38.4 all-gather.1

commit v2 on v1

v2 whole, which is shorter than its diff:
```python
import functools

import jax
import jax.numpy as jnp
from jax import lax
from jax.experimental import pallas as pl
from jax.experimental.pallas import tpu as pltpu
from jax.sharding import PartitionSpec as P

VMEM = pltpu.VMEM
SMEM = pltpu.SMEM
DMA = pltpu.SemaphoreType.DMA
F32 = jnp.float32
BF16 = jnp.bfloat16
I16 = jnp.int16
I32 = jnp.int32
LEVELS = 32767.0
STEPS = 256.0
TINY = 1e-37


def split(x):
    hi = x.astype(BF16)
    return hi, (x - hi.astype(F32)).astype(BF16)


def encode(x):
    size = jnp.abs(x)
    down = jnp.zeros_like(x)
    for k in (64, 32, 16, 8, 4, 2, 1):
        small = size < 2.0**-k
        size = jnp.where(small, size * 2.0**k, size)
        down = jnp.where(small, down + k, down)
    digits = jnp.where(x < 0, -256.0, 256.0) * size
    return ((63.0 - down) * 512.0 + digits + 256.0).astype(I32)


def decode(code):
    power = (code >> 9).astype(F32)
    digits = ((code & 511) - 256).astype(F32)
    return digits * jnp.exp2(power - 71.0)


def prep_kernel(
    width, wave, slope, hop, off, cnt, bond, shift, vp,
    own_ref, pay_ref, hop_out, phase_out,
    wave_v, slope_v, hop_v, bond_v, shift_v, cnt_s, vp_s, sems,
):
    blocks, slots, rows, _ = hop.shape
    pairs = ((hop, hop_v), (bond, bond_v), (shift, shift_v), (cnt, cnt_s), (vp, vp_s), (wave, wave_v), (slope, slope_v))
    copies = [pltpu.make_async_copy(a, b, sems.at[n]) for n, (a, b) in enumerate(pairs)]
    for copy in copies:
        copy.start()
    copies[0].wait()
    for i in range(blocks):
        line = jnp.concatenate([hop_v[i, s].astype(F32) for s in range(slots)], axis=1)
        hop_out[i] = encode(line).astype(I16)
    for copy in copies[1:5]:
        copy.wait()
    theta = jnp.zeros((blocks, slots), F32)
    for k in range(3):
        theta = theta + vp_s[k] * (bond_v[k] + 2.0 * shift_v[k].astype(F32))
    row = lax.broadcasted_iota(I32, (blocks, slots), 0)
    slot = lax.broadcasted_iota(I32, (blocks, slots), 1)
    count = jnp.zeros((blocks, slots), I32)
    for i in range(blocks):
        count = jnp.where(row == i, cnt_s[i], count)
    live = slot < count
    phase_out[0:blocks] = jnp.where(live, jnp.cos(theta), 0.0)
    phase_out[blocks:] = jnp.where(live, jnp.sin(theta), 0.0)
    for copy in copies[5:]:
        copy.wait()
    codes = []
    for c in range(blocks * width // 128):
        cols = pl.ds(c * 128, 128)
        seg = wave_v[:, :, cols] + 0.25 * slope_v[:, :, cols]
        both = jnp.concatenate([seg[0].T, seg[1].T], axis=1)
        hi, lo = split(both)
        for k in range(128 // width):
            j = c * (128 // width) + k
            part = both[k * width : (k + 1) * width]
            own_ref[j, 0:width] = hi[k * width : (k + 1) * width]
            own_ref[j, width : 2 * width] = lo[k * width : (k + 1) * width]
            top = jnp.maximum(jnp.max(jnp.abs(part), axis=0, keepdims=True), TINY)
            code = jnp.ceil(jnp.log2(top) * STEPS) + 1.0
            codes.append(code)
            q = jnp.round(part * (LEVELS * jnp.exp2(code * (-1.0 / STEPS))))
            pay_ref[j * width : (j + 1) * width] = q.astype(I32).astype(I16)
    pay_ref[blocks * width :] = jnp.concatenate(codes, axis=0).astype(I32).astype(I16)


def slots_kernel(hop_ref, own_ref, prev_ref, next_ref, phase, off, out, xs, out_v, phase_s, off_s, sems, out_sems):
    blocks, rows, depth = hop_ref.shape
    slots = off.shape[1]
    width = depth // slots
    states = out.shape[1]
    phase_copy = pltpu.make_async_copy(phase, phase_s, sems.at[0])
    off_copy = pltpu.make_async_copy(off, off_s, sems.at[1])
    phase_copy.start()
    off_copy.start()

    for j in range(blocks):
        xs[blocks + j] = own_ref[j]
    for base, ref in ((0, prev_ref), (2 * blocks, next_ref)):
        code = ref[blocks * width :].astype(I32).astype(F32)
        scale = jnp.exp2(code * (1.0 / STEPS)) * (1.0 / LEVELS)
        for j in range(blocks):
            q = ref[j * width : (j + 1) * width].astype(I32).astype(F32)
            hi, lo = split(q * scale[j : j + 1])
            xs[base + j, 0:width] = hi
            xs[base + j, width : 2 * width] = lo
    phase_copy.wait()
    off_copy.wait()

    def out_copy(pair):
        cols = pl.ds(pl.multiple_of(pair * 2 * rows, 2 * rows), 2 * rows)
        return pltpu.make_async_copy(out_v.at[:, :, cols], out.at[:, :, cols], out_sems.at[pair])

    def block_pair(pair, _):
        res = []
        for k in range(2):
            i = 2 * pair + k
            a = jnp.zeros((rows, 2 * states), F32)
            b = jnp.zeros((rows, 2 * states), F32)
            for p in range(slots // 2):
                tile = decode(hop_ref[i, :, 2 * width * p : 2 * width * (p + 1)].astype(I32)).astype(BF16)
                for h in range(2):
                    s = 2 * p + h
                    half = tile[:, h * width : (h + 1) * width]
                    prod = jnp.dot(
                        jnp.concatenate([half, half], axis=1),
                        xs[off_s[i, s] + (i + blocks)],
                        preferred_element_type=F32,
                    )
                    a = a + phase_s[i, s] * prod
                    b = b + phase_s[blocks + i, s] * prod
            res.append((a[:, states:] + b[:, :states], b[:, states:] - a[:, :states]))
        cols = pl.ds(pl.multiple_of(pair * 2 * rows, 2 * rows), 2 * rows)
        out_v[0, :, cols] = jnp.concatenate([res[0][0], res[1][0]], axis=0).T
        out_v[1, :, cols] = jnp.concatenate([res[0][1], res[1][1]], axis=0).T
        out_copy(pair).start()
        return 0

    lax.fori_loop(0, blocks // 2, block_pair, 0)
    for pair in range(blocks // 2):
        out_copy(pair).wait()


def on_device(
    wavefunction, slope_prev, hopping, offsets, counts, bond_vectors, shifts, vector_potential
):
    blocks, slots, rows, width = hopping.shape
    states = wavefunction.shape[1]
    orbs = blocks * width
    vm = pl.BlockSpec(memory_space=VMEM)
    far = pl.BlockSpec(memory_space=pltpu.HBM)
    own, payload, part, phase = pl.pallas_call(
        functools.partial(prep_kernel, width),
        out_shape=(
            jax.ShapeDtypeStruct((blocks, 2 * width, 2 * states), BF16),
            jax.ShapeDtypeStruct((orbs + blocks, 2 * states), I16),
            jax.ShapeDtypeStruct((blocks, rows, slots * width), I16),
            jax.ShapeDtypeStruct((2 * blocks, slots), F32),
        ),
        in_specs=[far] * 8,
        out_specs=[vm] * 4,
        scratch_shapes=[
            VMEM(wavefunction.shape, F32),
            VMEM(slope_prev.shape, F32),
            VMEM(hopping.shape, BF16),
            VMEM(bond_vectors.shape, F32),
            VMEM(shifts.shape, I32),
            SMEM(counts.shape, I32),
            SMEM(vector_potential.shape, F32),
            DMA((7,)),
        ],
        compiler_params=pltpu.CompilerParams(vmem_limit_bytes=64 * 1024 * 1024),
        name="prep",
    )(wavefunction, slope_prev, hopping, offsets, counts, bond_vectors, shifts, vector_potential)
    size = lax.axis_size("orb")
    up = [(i, (i + 1) % size) for i in range(size)]
    down = [(j, i) for i, j in up]
    before = lax.ppermute(payload, "orb", up)
    after = lax.ppermute(payload, "orb", down)
    tiles = lax.all_gather(part, "st", axis=1, tiled=True)
    return pl.pallas_call(
        slots_kernel,
        out_shape=jax.ShapeDtypeStruct((2, states, orbs), F32),
        in_specs=[vm] * 4 + [far] * 2,
        out_specs=far,
        scratch_shapes=[
            VMEM((3 * blocks, 2 * width, 2 * states), BF16),
            VMEM((2, states, orbs), F32),
            SMEM((2 * blocks, slots), F32),
            SMEM((blocks, slots), I32),
            DMA((2,)),
            DMA((blocks // 2,)),
        ],
        compiler_params=pltpu.CompilerParams(vmem_limit_bytes=40 * 1024 * 1024),
        name="slots",
    )(tiles, own, before, after, phase, offsets)


def solution(mesh):
    return jax.shard_map(
        on_device,
        mesh=mesh,
        in_specs=(
            P(None, "st", "orb"),
            P(None, "st", "orb"),
            P("orb", None, "st", None),
            P("orb", None),
            P("orb"),
            P(None, "orb", None),
            P(None, "orb", None),
            P(),
        ),
        out_specs=P(None, "st", "orb"),
        check_vma=False,
    )
```

time: 66.8 us -> 43.1 us (0.65)
  waiting for transfers between devices: 19.4 us -> 0.01 us
  blocking collectives: 0 us -> 16.7 us
  between operations: 13.4 us -> 0.07 us
  local copies, waits for them, and re-layouts: 8.52 us -> 0.02 us
  Pallas kernels: 8.63 us -> 9.75 us
    all_gather x0 -> x1, blocking collectives: none -> 16.7 us  [on_device(): tiles = lax.all_gather(part, 'st', axis=1, tiled=True)]
    ppermute x1, waiting for transfers between devices: 8.82 us -> 0.01 us  [on_device(): after = lax.ppermute(payload, 'orb', down)]
    unnamed x16 -> x6, local copies, waits for them, and re-layouts: 7.79 us -> 0.02 us
    ppermute x1, waiting for transfers between devices: 7.12 us -> 0.01 us  [on_device(): before = lax.ppermute(payload, 'orb', up)]
    all_gather x1 -> x0, waiting for transfers between devices: 3.43 us -> none  [on_device(): tiles = lax.all_gather(part, 'st', axis=1, tiled=True)]
    pallas_call x2 -> x1, Pallas kernels: 1.84 us -> 3.53 us  [on_device(): pl.pallas_call(functools.partial(prep_kernel, width), out_shape=(jax.Shap...]
    broadcast_in_dim x1 -> x0, local copies, waits for them, and re-layouts: 0.73 us -> none  [on_device(): counts[:, None]]
  transfers between devices with their start and end apart: 3 -> 2, of which waited for: 3 -> 0; matrix products, arithmetic and copies ran while one was open for 0% -> 0% of each run, Pallas kernels for 1% -> 0%
where the time goes in v2:
time: 43.1 us; the launch traced here: 43 us
  blocking collectives  16.7 us (39%)
  starting transfers between devices  16.5 us (38%)
  Pallas kernels  9.75 us (23%)
    all_gather x1, blocking collectives, on_device(): tiles = lax.all_gather(part, 'st', axis=1, tiled=True)  16.7 us
    ppermute x1, starting transfers between devices, on_device(): after = lax.ppermute(payload, 'orb', down)  14.5 us
    pallas_call x1, Pallas kernels, on_device(): pl.pallas_call(slots_kernel, out_shape=jax.ShapeDtypeStruct((2, states, o...  6.22 us
    pallas_call x1, Pallas kernels, on_device(): pl.pallas_call(functools.partial(prep_kernel, width), out_shape=(jax.Shap...  3.53 us
    ppermute x1, starting transfers between devices, on_device(): before = lax.ppermute(payload, 'orb', up)  1.92 us
  transfers between devices with their start and end apart: 2, of which 0 were waited for; matrix products, arithmetic and copies ran while one was open for 0% of the time, Pallas kernels for 0%

profile of v2, /device:TPU:1, one launch (start us, length us, event | category | flops | bytes accessed | tf_op | source)
XLA Modules:
  0.0 43.0 jit_solution(5465635676692333699)
XLA Ops:
  0.0 3.5 %prep.1 = (bf16[16,128,256]{2,1,0:T(8,128)(2,1)}, s16[1040,256]{1,0:T(8,128)(2,1)}, s16[16,8,896]{2,1,0:T(8,128)(2,1)}, f32[32,14]{1,0:T(8,128)}) custom-call(f32[2,128,1024]{2,1,0:T(8,128)} %wave.1, f32[2,128,1024]{2,1,0:T(8,128)} %slope.1, bf16[16,14,8,64]{3,2,1,0:T(8,128)(2,1)} %hop.1, s32[16,14]{1,0:T(8,128)} %off.3, s32[16]{0:T(128)} %cnt.1, ...), custom_call_target="tpu_custom_call" | custom-call | tf_op jit(solution)/shard_map/prep/pallas_call | solution.py:157
  3.5 0.0 copy-start
  3.6 0.0 copy-start.1
  3.6 0.0 copy-start.2
  3.6 14.5 %collective-permute-start.1 = (s16[1040,256]{1,0:T(8,128)(2,1)}, s16[1040,256]{1,0:T(8,128)(2,1)S(1)}, u32[]{:S(2)}, u32[]{:S(2)}) collective-permute-start(s16[1040,256]{1,0:T(8,128)(2,1)} %get-tuple-element.11), channel_id=1, source_target_pairs={{8,0},{16,8},{24,16},{32,24},{40,32},{48,40},{56,48},{64,56},{72,6... | collective-permute-start | bytes 1597448 | tf_op jit(solution)/shard_map/ppermute | solution.py:184
  18.1 1.9 %collective-permute-start = (s16[1040,256]{1,0:T(8,128)(2,1)}, s16[1040,256]{1,0:T(8,128)(2,1)S(1)}, u32[]{:S(2)}, u32[]{:S(2)}) collective-permute-start(s16[1040,256]{1,0:T(8,128)(2,1)} %get-tuple-element.11), channel_id=1, source_target_pairs={{0,8},{8,16},{16,24},{24,32},{32,40},{40,48},{48,56},{56,64},{64,7... | collective-permute-start | bytes 1597448 | tf_op jit(solution)/shard_map/ppermute | solution.py:183
  20.0 16.7 %all-gather.1.hop_ref = s16[16,64,896]{2,1,0:T(8,128)(2,1)S(1)} all-gather(s16[16,8,896]{2,1,0:T(8,128)(2,1)} %get-tuple-element.9), channel_id=1, replica_groups=mesh['orb'=64,'st'=8] {'st'}, dimensions={1}, use_global_device_ids=true | all-gather | bytes 2064384 | tf_op jit(solution)/shard_map/all_gather | solution.py:185
  36.7 0.0 collective-permute-done.1.next_ref
  36.7 0.0 collective-permute-done.prev_ref
  36.7 0.0 copy-done
  36.7 0.0 copy-done.1
  36.7 0.0 copy-done.2
  36.8 6.2 %slots.1 = f32[2,128,1024]{2,1,0:T(8,128)} custom-call(s16[16,64,896]{2,1,0:T(8,128)(2,1)S(1)} %all-gather.1.hop_ref, bf16[16,128,256]{2,1,0:T(8,128)(2,1)S(1)} %copy-done, s16[1040,256]{1,0:T(8,128)(2,1)S(1)} %collective-permute-done.prev_ref, s16[1040,256]{1,0:T(8,128)(2,1)S(1)} %collective-permute-done.1.next_ref, f32[32,14]{1,0:T(8,128)S(1)} %copy-done.2, ...), custom_call_target="tpu_custom_call" | custom-call | tf_op jit(solution)/shard_map/slots/pallas_call | solution.py:186
Async XLA Ops:
  3.5 33.2 %copy-start = (bf16[16,128,256]{2,1,0:T(8,128)(2,1)S(1)}, bf16[16,128,256]{2,1,0:T(8,128)(2,1)}, u32[]{:S(2)}) copy-start(bf16[16,128,256]{2,1,0:T(8,128)(2,1)} %get-tuple-element.10.own_ref) | copy-start | bytes 3145732
  3.6 33.2 %copy-start.1 = (s32[16,14]{1,0:T(8,128)S(1)}, s32[16,14]{1,0:T(8,128)}, u32[]{:S(2)}) copy-start(s32[16,14]{1,0:T(8,128)} %off.3) | copy-start | bytes 2692
  3.6 33.2 %copy-start.2 = (f32[32,14]{1,0:T(8,128)S(1)}, f32[32,14]{1,0:T(8,128)}, u32[]{:S(2)}) copy-start(f32[32,14]{1,0:T(8,128)} %get-tuple-element.12.phase) | copy-start | bytes 5380
  3.6 33.1 %collective-permute-start.1 = (s16[1040,256]{1,0:T(8,128)(2,1)}, s16[1040,256]{1,0:T(8,128)(2,1)S(1)}, u32[]{:S(2)}, u32[]{:S(2)}) collective-permute-start(s16[1040,256]{1,0:T(8,128)(2,1)} %get-tuple-element.11), channel_id=1, source_target_pairs={{8,0},{16,8},{24,16},{32,24},{40,32},{48,40},{56,48},{64,56},{72,6... | collective-permute-start | bytes 1597448 | tf_op jit(solution)/shard_map/ppermute | solution.py:184
  18.1 18.6 %collective-permute-start = (s16[1040,256]{1,0:T(8,128)(2,1)}, s16[1040,256]{1,0:T(8,128)(2,1)S(1)}, u32[]{:S(2)}, u32[]{:S(2)}) collective-permute-start(s16[1040,256]{1,0:T(8,128)(2,1)} %get-tuple-element.11), channel_id=1, source_target_pairs={{0,8},{8,16},{16,24},{24,32},{32,40},{40,48},{48,56},{56,64},{64,7... | collective-permute-start | bytes 1597448 | tf_op jit(solution)/shard_map/ppermute | solution.py:183

commit v3 on v2

v3 whole, which is shorter than its diff:
```python
import functools

import jax
import jax.numpy as jnp
from jax import lax
from jax.experimental import pallas as pl
from jax.experimental.pallas import tpu as pltpu
from jax.sharding import PartitionSpec as P

VMEM = pltpu.VMEM
SMEM = pltpu.SMEM
DMA = pltpu.SemaphoreType.DMA
F32 = jnp.float32
BF16 = jnp.bfloat16
I16 = jnp.int16
I32 = jnp.int32
LEVELS = 32767.0
STEPS = 256.0
TINY = 1e-37
UP = 71


def split(x):
    hi = x.astype(BF16)
    return hi, (x - hi.astype(F32)).astype(BF16)


def encode(x):
    size = jnp.maximum(jnp.abs(x), TINY)
    down = jnp.floor(-0.0028 - jnp.log2(size))
    digits = jnp.round(x * jnp.exp2(down) * 256.0)
    return (digits * 128.0 + (127.0 - down)).astype(I32).astype(I16)


def decode(code):
    code = jnp.concatenate([x.astype(I32) for x in code], axis=0)
    digits = (code >> 7).astype(F32).astype(BF16)
    return digits * jnp.exp2((code & 127).astype(F32).astype(BF16) - jnp.bfloat16(64))


def tiles_kernel(hop, cnt, bond, shift, vp, part, phase):
    blocks, slots, rows, _ = hop.shape
    for i in range(blocks):
        line = jnp.concatenate([hop[i, s].astype(F32) for s in range(slots)], axis=1)
        part[i] = encode(line)
    theta = jnp.zeros((blocks, slots), F32)
    for k in range(3):
        theta = theta + vp[0:1, k : k + 1] * (bond[k] + 2.0 * shift[k].astype(F32))
    slot = lax.broadcasted_iota(I32, (blocks, blocks), 0)
    live = jnp.where(slot < cnt[...], 2.0**-UP, 0.0).T[:, 0:slots]
    phase[0:blocks] = live * jnp.cos(theta)
    phase[blocks:] = live * jnp.sin(theta)


def segment_kernel(width, wave, slope, own, pay, wave_v, slope_v, sems):
    orbs = wave.shape[2]
    chunk = 256
    copies = []
    for at in range(0, orbs, chunk):
        span = pl.ds(at, chunk)
        for x, x_v in ((wave, wave_v), (slope, slope_v)):
            copies.append(pltpu.make_async_copy(x.at[:, :, span], x_v.at[:, :, span], sems.at[len(copies)]))
            copies[-1].start()
    codes = []
    for c in range(0, orbs, 128):
        if c % chunk == 0:
            for copy in copies[2 * (c // chunk) :][:2]:
                copy.wait()
        cols = pl.ds(c, 128)
        seg = wave_v[:, :, cols] + 0.25 * slope_v[:, :, cols]
        both = jnp.concatenate([seg[0].T, seg[1].T], axis=1)
        hi, lo = split(both)
        for k in range(128 // width):
            j = c // width + k
            span = slice(k * width, (k + 1) * width)
            own[j, 0:width] = hi[span]
            own[j, width : 2 * width] = lo[span]
            top = jnp.maximum(jnp.max(jnp.abs(both[span]), axis=0, keepdims=True), TINY)
            code = jnp.ceil(jnp.log2(top) * STEPS) + 1.0
            codes.append(code)
            q = jnp.round(both[span] * (LEVELS * jnp.exp2(code * (-1.0 / STEPS))))
            pay[j * width : (j + 1) * width] = q.astype(I32).astype(I16)
    pay[orbs:] = jnp.concatenate(codes, axis=0).astype(I32).astype(I16)


def slots_kernel(hop_ref, own_ref, prev_ref, next_ref, phase, off, out, xs, out_v, phase_s, off_s, sems, out_sems):
    peers, blocks, group, depth = hop_ref.shape
    rows = peers * group
    slots = off.shape[1]
    width = depth // slots
    states = out.shape[1]
    phase_copy = pltpu.make_async_copy(phase, phase_s, sems.at[0])
    off_copy = pltpu.make_async_copy(off, off_s, sems.at[1])
    phase_copy.start()
    off_copy.start()

    for j in range(blocks):
        xs[blocks + j] = own_ref[j]
    for base, ref in ((0, prev_ref), (2 * blocks, next_ref)):
        code = ref[blocks * width :].astype(I32).astype(F32)
        scale = jnp.exp2(code * (1.0 / STEPS)) * (1.0 / LEVELS)
        for j in range(blocks):
            q = ref[j * width : (j + 1) * width].astype(I32).astype(F32)
            hi, lo = split(q * scale[j : j + 1])
            xs[base + j, 0:width] = hi
            xs[base + j, width : 2 * width] = lo
    phase_copy.wait()
    off_copy.wait()

    def out_copy(pair):
        cols = pl.ds(pl.multiple_of(pair * 2 * rows, 2 * rows), 2 * rows)
        return pltpu.make_async_copy(out_v.at[:, :, cols], out.at[:, :, cols], out_sems.at[pair])

    def block_pair(pair, _):
        res = []
        for k in range(2):
            i = 2 * pair + k
            a = jnp.zeros((rows, 2 * states), F32)
            b = jnp.zeros((rows, 2 * states), F32)
            for p in range(slots // 2):
                tile = decode([hop_ref[n, i, :, 2 * width * p : 2 * width * (p + 1)] for n in range(peers)])
                for h in range(2):
                    s = 2 * p + h
                    half = tile[:, h * width : (h + 1) * width]
                    prod = jnp.dot(
                        jnp.concatenate([half, half], axis=1),
                        xs[off_s[i, s] + (i + blocks)],
                        preferred_element_type=F32,
                    )
                    a = a + phase_s[i, s] * prod
                    b = b + phase_s[blocks + i, s] * prod
            res.append((a[:, states:] + b[:, :states], b[:, states:] - a[:, :states]))
        cols = pl.ds(pl.multiple_of(pair * 2 * rows, 2 * rows), 2 * rows)
        out_v[0, :, cols] = jnp.concatenate([res[0][0], res[1][0]], axis=0).T
        out_v[1, :, cols] = jnp.concatenate([res[0][1], res[1][1]], axis=0).T
        out_copy(pair).start()
        return 0

    lax.fori_loop(0, blocks // 2, block_pair, 0, unroll=True)
    for pair in range(blocks // 2):
        out_copy(pair).wait()


def on_device(
    wavefunction, slope_prev, hopping, offsets, counts, bond_vectors, shifts, vector_potential
):
    blocks, slots, rows, width = hopping.shape
    states = wavefunction.shape[1]
    orbs = blocks * width
    vm = pl.BlockSpec(memory_space=VMEM)
    far = pl.BlockSpec(memory_space=pltpu.HBM)
    own, payload = pl.pallas_call(
        functools.partial(segment_kernel, width),
        out_shape=(
            jax.ShapeDtypeStruct((blocks, 2 * width, 2 * states), BF16),
            jax.ShapeDtypeStruct((orbs + blocks, 2 * states), I16),
        ),
        in_specs=[far] * 2,
        out_specs=[vm] * 2,
        scratch_shapes=[VMEM(wavefunction.shape, F32), VMEM(slope_prev.shape, F32), DMA((orbs // 128,))],
        compiler_params=pltpu.CompilerParams(vmem_limit_bytes=52 * 1024 * 1024),
        name="segment",
    )(wavefunction, slope_prev)
    part, phase = pl.pallas_call(
        tiles_kernel,
        out_shape=(
            jax.ShapeDtypeStruct((blocks, rows, slots * width), I16),
            jax.ShapeDtypeStruct((2 * blocks, slots), F32),
        ),
        in_specs=[vm] * 5,
        out_specs=[vm] * 2,
        compiler_params=pltpu.CompilerParams(vmem_limit_bytes=40 * 1024 * 1024),
        name="tiles",
    )(hopping, counts[None], bond_vectors, shifts, vector_potential[None])
    size = lax.axis_size("orb")
    up = [(i, (i + 1) % size) for i in range(size)]
    down = [(j, i) for i, j in up]
    before = lax.ppermute(payload, "orb", up)
    after = lax.ppermute(payload, "orb", down)
    tiles = lax.all_gather(part, "st")
    return pl.pallas_call(
        slots_kernel,
        out_shape=jax.ShapeDtypeStruct((2, states, orbs), F32),
        in_specs=[vm] * 4 + [far] * 2,
        out_specs=far,
        scratch_shapes=[
            VMEM((3 * blocks, 2 * width, 2 * states), BF16),
            VMEM((2, states, orbs), F32),
            SMEM((2 * blocks, slots), F32),
            SMEM((blocks, slots), I32),
            DMA((2,)),
            DMA((blocks // 2,)),
        ],
        compiler_params=pltpu.CompilerParams(vmem_limit_bytes=40 * 1024 * 1024),
        name="slots",
    )(tiles, own, before, after, phase, offsets)


def solution(mesh):
    return jax.shard_map(
        on_device,
        mesh=mesh,
        in_specs=(
            P(None, "st", "orb"),
            P(None, "st", "orb"),
            P("orb", None, "st", None),
            P("orb", None),
            P("orb"),
            P(None, "orb", None),
            P(None, "orb", None),
            P(),
        ),
        out_specs=P(None, "st", "orb"),
        check_vma=False,
    )
```

time: 43.1 us -> 40 us (0.928)
  Pallas kernels: 9.75 us -> 7.45 us
  blocking collectives: 16.7 us -> 15.9 us
    pallas_call x1 -> x2, Pallas kernels: 3.53 us -> 2.26 us  [the longest x1 1.88 us: on_device(): pl.pallas_call(functools.partial(segment_kernel, width), out_shape=(jax.S...]
    pallas_call x1, Pallas kernels: 6.22 us -> 5.19 us  [on_device(): pl.pallas_call(slots_kernel, out_shape=jax.ShapeDtypeStruct((2, states, o...]
    all_gather x1, blocking collectives: 16.7 us -> 15.9 us  [on_device(): tiles = lax.all_gather(part, 'st')]
  transfers between devices with their start and end apart: 2 -> 2, of which waited for: 0 -> 0; matrix products, arithmetic and copies ran while one was open for 0% -> 0% of each run, Pallas kernels for 0% -> 1%
where the time goes in v3:
time: 40 us; the launch traced here: 39.8 us
  starting transfers between devices  16.3 us (41%)
  blocking collectives  15.9 us (40%)
  Pallas kernels  7.45 us (19%)
    all_gather x1, blocking collectives, on_device(): tiles = lax.all_gather(part, 'st')  15.9 us
    ppermute x1, starting transfers between devices, on_device(): after = lax.ppermute(payload, 'orb', down)  14.4 us
    pallas_call x1, Pallas kernels, on_device(): pl.pallas_call(slots_kernel, out_shape=jax.ShapeDtypeStruct((2, states, o...  5.19 us
    ppermute x1, starting transfers between devices, on_device(): before = lax.ppermute(payload, 'orb', up)  1.92 us
    pallas_call x1, Pallas kernels, on_device(): pl.pallas_call(functools.partial(segment_kernel, width), out_shape=(jax.S...  1.88 us
  transfers between devices with their start and end apart: 2, of which 0 were waited for; matrix products, arithmetic and copies ran while one was open for 0% of the time, Pallas kernels for 1%

profile of v3, /device:TPU:1, one launch (start us, length us, event | category | flops | bytes accessed | tf_op | source)
XLA Modules:
  0.0 39.8 jit_solution(4800620016438863711)
XLA Ops:
  0.0 0.0 copy-start.5
  0.0 0.0 copy-start.2
  0.0 0.0 copy-start.1
  0.0 0.0 copy-start.4
  0.0 0.0 copy-start
  0.0 0.0 copy-start.3
  0.0 1.9 %segment.1 = (bf16[16,128,256]{2,1,0:T(8,128)(2,1)S(1)}, s16[1040,256]{1,0:T(8,128)(2,1)S(1)}) custom-call(f32[2,128,1024]{2,1,0:T(8,128)} %wave.1, f32[2,128,1024]{2,1,0:T(8,128)} %slope.1), custom_call_target="tpu_custom_call" | custom-call | tf_op jit(solution)/shard_map/segment/pallas_call | solution.py:152
  1.9 14.4 %collective-permute-start.1 = (s16[1040,256]{1,0:T(8,128)(2,1)S(1)}, s16[1040,256]{1,0:T(8,128)(2,1)S(1)}, u32[]{:S(2)}, u32[]{:S(2)}) collective-permute-start(s16[1040,256]{1,0:T(8,128)(2,1)S(1)} %get-tuple-element.11), channel_id=1, source_target_pairs={{8,0},{16,8},{24,16},{32,24},{40,32},{48,40},{56,48},{64,56},{72,6... | collective-permute-start | bytes 1597448 | tf_op jit(solution)/shard_map/ppermute | solution.py:179
  16.3 1.9 %collective-permute-start = (s16[1040,256]{1,0:T(8,128)(2,1)S(1)}, s16[1040,256]{1,0:T(8,128)(2,1)S(1)}, u32[]{:S(2)}, u32[]{:S(2)}) collective-permute-start(s16[1040,256]{1,0:T(8,128)(2,1)S(1)} %get-tuple-element.11), channel_id=1, source_target_pairs={{0,8},{8,16},{16,24},{24,32},{32,40},{40,48},{48,56},{56,64},{64,7... | collective-permute-start | bytes 1597448 | tf_op jit(solution)/shard_map/ppermute | solution.py:178
  18.3 0.0 copy-done.5
  18.3 0.0 copy-done.2
  18.3 0.0 copy-done.1
  18.3 0.0 copy-done.4
  18.3 0.0 copy-done
  18.3 0.4 tiles.1
  18.7 15.9 %all-gather.2 = s16[128,8,896]{2,1,0:T(8,128)(2,1)S(1)} all-gather(s16[16,8,896]{2,1,0:T(8,128)(2,1)S(1)} %get-tuple-element.9), channel_id=2, replica_groups=mesh['orb'=64,'st'=8] {'st'}, dimensions={0}, use_global_device_ids=true | all-gather | bytes 2064384 | tf_op jit(solution)/shard_map/all_gather | solution.py:180
  34.6 0.0 collective-permute-done.1.next_ref
  34.6 0.0 collective-permute-done.prev_ref
  34.6 0.0 copy-done.3
  34.6 5.2 %slots.1 = f32[2,128,1024]{2,1,0:T(8,128)} custom-call(s16[8,16,8,896]{3,2,1,0:T(8,128)(2,1)S(1)} %bitcast.3, bf16[16,128,256]{2,1,0:T(8,128)(2,1)S(1)} %get-tuple-element.10.own_ref, s16[1040,256]{1,0:T(8,128)(2,1)S(1)} %collective-permute-done.prev_ref, s16[1040,256]{1,0:T(8,128)(2,1)S(1)} %collective-permute-done.1.next_ref, ...), custom_call_target="tpu_custom_call" | custom-call | tf_op jit(solution)/shard_map/slots/pallas_call | solution.py:181
Async XLA Ops:
  0.0 18.3 %copy-start.5 = (f32[3]{0:T(128)S(1)}, f32[3]{0:T(128)}, u32[]{:S(2)}) copy-start(f32[3]{0:T(128)} %param.15) | copy-start | bytes 40
  0.0 18.3 %copy-start.2 = (s32[3,16,14]{2,1,0:T(8,128)S(1)}, s32[3,16,14]{2,1,0:T(8,128)}, u32[]{:S(2)}) copy-start(s32[3,16,14]{2,1,0:T(8,128)} %shift.1) | copy-start | bytes 8068
  0.0 18.3 %copy-start.1 = (f32[3,16,14]{2,1,0:T(8,128)S(1)}, f32[3,16,14]{2,1,0:T(8,128)}, u32[]{:S(2)}) copy-start(f32[3,16,14]{2,1,0:T(8,128)} %bond.1) | copy-start | bytes 8068
  0.0 18.3 %copy-start.4 = (s32[16]{0:T(128)S(1)}, s32[16]{0:T(128)}, u32[]{:S(2)}) copy-start(s32[16]{0:T(128)} %param.12) | copy-start | bytes 196
  0.0 18.3 %copy-start = (bf16[16,14,8,64]{3,2,1,0:T(8,128)(2,1)S(1)}, bf16[16,14,8,64]{3,2,1,0:T(8,128)(2,1)}, u32[]{:S(2)}) copy-start(bf16[16,14,8,64]{3,2,1,0:T(8,128)(2,1)} %hop.1) | copy-start | bytes 688132
  0.0 34.6 %copy-start.3 = (s32[16,14]{1,0:T(8,128)S(1)}, s32[16,14]{1,0:T(8,128)}, u32[]{:S(2)}) copy-start(s32[16,14]{1,0:T(8,128)} %off.1) | copy-start | bytes 2692
  1.9 32.7 %collective-permute-start.1 = (s16[1040,256]{1,0:T(8,128)(2,1)S(1)}, s16[1040,256]{1,0:T(8,128)(2,1)S(1)}, u32[]{:S(2)}, u32[]{:S(2)}) collective-permute-start(s16[1040,256]{1,0:T(8,128)(2,1)S(1)} %get-tuple-element.11), channel_id=1, source_target_pairs={{8,0},{16,8},{24,16},{32,24},{40,32},{48,40},{56,48},{64,56},{72,6... | collective-permute-start | bytes 1597448 | tf_op jit(solution)/shard_map/ppermute | solution.py:179
  16.3 18.3 %collective-permute-start = (s16[1040,256]{1,0:T(8,128)(2,1)S(1)}, s16[1040,256]{1,0:T(8,128)(2,1)S(1)}, u32[]{:S(2)}, u32[]{:S(2)}) collective-permute-start(s16[1040,256]{1,0:T(8,128)(2,1)S(1)} %get-tuple-element.11), channel_id=1, source_target_pairs={{0,8},{8,16},{16,24},{24,32},{32,40},{40,48},{48,56},{56,64},{64,7... | collective-permute-start | bytes 1597448 | tf_op jit(solution)/shard_map/ppermute | solution.py:178

commit v4 on v3

--- a/solution.py
+++ b/solution.py
@@ -83,7 +83,7 @@
     pay[orbs:] = jnp.concatenate(codes, axis=0).astype(I32).astype(I16)
 
 
-def slots_kernel(hop_ref, own_ref, prev_ref, next_ref, phase, off, out, xs, out_v, phase_s, off_s, sems, out_sems):
+def slots_kernel(hop_ref, own_ref, next_ref, prev_ref, phase, off, out, xs, tiles_v, out_v, phase_s, off_s, sems, out_sems):
     peers, blocks, group, depth = hop_ref.shape
     rows = peers * group
     slots = off.shape[1]
@@ -104,41 +104,40 @@
             hi, lo = split(q * scale[j : j + 1])
             xs[base + j, 0:width] = hi
             xs[base + j, width : 2 * width] = lo
+    def left(i, s):
+        span = pl.ds(width * (s - s % 2), 2 * width)
+        tile = decode([hop_ref[n, i, :, span] for n in range(peers)])
+        half = tile[:, s % 2 * width : (s % 2 + 1) * width]
+        return jnp.concatenate([half, half], axis=1)
+
+    early = tiles_v.shape[0]
+    for i in range(early):
+        for s in range(slots):
+            tiles_v[i, s] = left(i, s)
     phase_copy.wait()
     off_copy.wait()
-
-    def out_copy(pair):
-        cols = pl.ds(pl.multiple_of(pair * 2 * rows, 2 * rows), 2 * rows)
-        return pltpu.make_async_copy(out_v.at[:, :, cols], out.at[:, :, cols], out_sems.at[pair])
-
-    def block_pair(pair, _):
+    copies = []
+    for pair in range(blocks // 2):
         res = []
-        for k in range(2):
-            i = 2 * pair + k
+        for i in (2 * pair, 2 * pair + 1):
             a = jnp.zeros((rows, 2 * states), F32)
             b = jnp.zeros((rows, 2 * states), F32)
-            for p in range(slots // 2):
-                tile = decode([hop_ref[n, i, :, 2 * width * p : 2 * width * (p + 1)] for n in range(peers)])
-                for h in range(2):
-                    s = 2 * p + h
-                    half = tile[:, h * width : (h + 1) * width]
-                    prod = jnp.dot(
-                        jnp.concatenate([half, half], axis=1),
-                        xs[off_s[i, s] + (i + blocks)],
-                        preferred_element_type=F32,
-                    )
-                    a = a + phase_s[i, s] * prod
-                    b = b + phase_s[blocks + i, s] * prod
+            for s in range(slots):
+                prod = jnp.dot(
+                    tiles_v[i, s] if i < early else left(i, s),
+                    xs[off_s[i, s] + (i + blocks)],
+                    preferred_element_type=F32,
+                )
+                a = a + phase_s[i, s] * prod
+                b = b + phase_s[blocks + i, s] * prod
             res.append((a[:, states:] + b[:, :states], b[:, states:] - a[:, :states]))
-        cols = pl.ds(pl.multiple_of(pair * 2 * rows, 2 * rows), 2 * rows)
+        cols = pl.ds(pair * 2 * rows, 2 * rows)
         out_v[0, :, cols] = jnp.concatenate([res[0][0], res[1][0]], axis=0).T
         out_v[1, :, cols] = jnp.concatenate([res[0][1], res[1][1]], axis=0).T
-        out_copy(pair).start()
-        return 0
-
-    lax.fori_loop(0, blocks // 2, block_pair, 0, unroll=True)
-    for pair in range(blocks // 2):
-        out_copy(pair).wait()
+        copies.append(pltpu.make_async_copy(out_v.at[:, :, cols], out.at[:, :, cols], out_sems.at[pair]))
+        copies[-1].start()
+    for copy in copies:
+        copy.wait()
 
 
 def on_device(
@@ -185,6 +184,7 @@
         out_specs=far,
         scratch_shapes=[
             VMEM((3 * blocks, 2 * width, 2 * states), BF16),
+            VMEM((4, slots, rows * lax.axis_size("st"), 2 * width), BF16),
             VMEM((2, states, orbs), F32),
             SMEM((2 * blocks, slots), F32),
             SMEM((blocks, slots), I32),
@@ -193,7 +193,7 @@
         ],
         compiler_params=pltpu.CompilerParams(vmem_limit_bytes=40 * 1024 * 1024),
         name="slots",
-    )(tiles, own, before, after, phase, offsets)
+    )(tiles, own, after, before, phase, offsets)
 
 
 def solution(mesh):

time: 40 us -> 39.6 us (0.990)
    ppermute x1, starting transfers between devices: 1.92 us -> 4.03 us  [on_device(): before = lax.ppermute(payload, 'orb', up)]
    ppermute x1, starting transfers between devices: 14.4 us -> 12.3 us  [on_device(): after = lax.ppermute(payload, 'orb', down)]
where the time goes in v4:
time: 39.6 us; the launch traced here: 39.4 us
  starting transfers between devices  16.3 us (41%)
  blocking collectives  15.9 us (40%)
  Pallas kernels  7.08 us (18%)
    all_gather x1, blocking collectives, on_device(): tiles = lax.all_gather(part, 'st')  15.9 us
    ppermute x1, starting transfers between devices, on_device(): after = lax.ppermute(payload, 'orb', down)  12.3 us
    pallas_call x1, Pallas kernels, on_device(): pl.pallas_call(slots_kernel, out_shape=jax.ShapeDtypeStruct((2, states, o...  4.82 us
    ppermute x1, starting transfers between devices, on_device(): before = lax.ppermute(payload, 'orb', up)  4.03 us
    pallas_call x1, Pallas kernels, on_device(): pl.pallas_call(functools.partial(segment_kernel, width), out_shape=(jax.S...  1.88 us
  transfers between devices with their start and end apart: 2, of which 0 were waited for; matrix products, arithmetic and copies ran while one was open for 0% of the time, Pallas kernels for 1%

profile of v4, /device:TPU:1, one launch (start us, length us, event | category | flops | bytes accessed | tf_op | source)
XLA Modules:
  0.0 39.4 jit_solution(4080202367185699864)
XLA Ops:
  0.0 0.0 copy-start.5
  0.0 0.0 copy-start.2
  0.0 0.0 copy-start.1
  0.0 0.0 copy-start.4
  0.0 0.0 copy-start
  0.0 0.0 copy-start.3
  0.0 1.9 %segment.1 = (bf16[16,128,256]{2,1,0:T(8,128)(2,1)S(1)}, s16[1040,256]{1,0:T(8,128)(2,1)S(1)}) custom-call(f32[2,128,1024]{2,1,0:T(8,128)} %wave.1, f32[2,128,1024]{2,1,0:T(8,128)} %slope.1), custom_call_target="tpu_custom_call" | custom-call | tf_op jit(solution)/shard_map/segment/pallas_call | solution.py:151
  1.9 4.0 %collective-permute-start.1 = (s16[1040,256]{1,0:T(8,128)(2,1)S(1)}, s16[1040,256]{1,0:T(8,128)(2,1)S(1)}, u32[]{:S(2)}, u32[]{:S(2)}) collective-permute-start(s16[1040,256]{1,0:T(8,128)(2,1)S(1)} %get-tuple-element.11), channel_id=1, source_target_pairs={{0,8},{8,16},{16,24},{24,32},{32,40},{40,48},{48,56},{56,64},{64,7... | collective-permute-start | bytes 1597448 | tf_op jit(solution)/shard_map/ppermute | solution.py:177
  6.0 12.3 %collective-permute-start = (s16[1040,256]{1,0:T(8,128)(2,1)S(1)}, s16[1040,256]{1,0:T(8,128)(2,1)S(1)}, u32[]{:S(2)}, u32[]{:S(2)}) collective-permute-start(s16[1040,256]{1,0:T(8,128)(2,1)S(1)} %get-tuple-element.11), channel_id=1, source_target_pairs={{8,0},{16,8},{24,16},{32,24},{40,32},{48,40},{56,48},{64,56},{72,6... | collective-permute-start | bytes 1597448 | tf_op jit(solution)/shard_map/ppermute | solution.py:178
  18.3 0.0 copy-done.5
  18.3 0.0 copy-done.2
  18.3 0.0 copy-done.1
  18.3 0.0 copy-done.4
  18.3 0.0 copy-done
  18.3 0.4 tiles.1
  18.7 15.9 %all-gather.2 = s16[128,8,896]{2,1,0:T(8,128)(2,1)S(1)} all-gather(s16[16,8,896]{2,1,0:T(8,128)(2,1)S(1)} %get-tuple-element.9), channel_id=2, replica_groups=mesh['orb'=64,'st'=8] {'st'}, dimensions={0}, use_global_device_ids=true | all-gather | bytes 2064384 | tf_op jit(solution)/shard_map/all_gather | solution.py:179
  34.6 0.0 collective-permute-done.1.prev_ref
  34.6 0.0 collective-permute-done.next_ref
  34.6 0.0 copy-done.3
  34.6 4.8 %slots.1 = f32[2,128,1024]{2,1,0:T(8,128)} custom-call(s16[8,16,8,896]{3,2,1,0:T(8,128)(2,1)S(1)} %bitcast.3, bf16[16,128,256]{2,1,0:T(8,128)(2,1)S(1)} %get-tuple-element.10.own_ref, s16[1040,256]{1,0:T(8,128)(2,1)S(1)} %collective-permute-done.next_ref, s16[1040,256]{1,0:T(8,128)(2,1)S(1)} %collective-permute-done.1.prev_ref, ...), custom_call_target="tpu_custom_call" | custom-call | tf_op jit(solution)/shard_map/slots/pallas_call | solution.py:180
Async XLA Ops:
  0.0 18.3 %copy-start.5 = (f32[3]{0:T(128)S(1)}, f32[3]{0:T(128)}, u32[]{:S(2)}) copy-start(f32[3]{0:T(128)} %param.15) | copy-start | bytes 40
  0.0 18.3 %copy-start.2 = (s32[3,16,14]{2,1,0:T(8,128)S(1)}, s32[3,16,14]{2,1,0:T(8,128)}, u32[]{:S(2)}) copy-start(s32[3,16,14]{2,1,0:T(8,128)} %shift.1) | copy-start | bytes 8068
  0.0 18.3 %copy-start.1 = (f32[3,16,14]{2,1,0:T(8,128)S(1)}, f32[3,16,14]{2,1,0:T(8,128)}, u32[]{:S(2)}) copy-start(f32[3,16,14]{2,1,0:T(8,128)} %bond.1) | copy-start | bytes 8068
  0.0 18.3 %copy-start.4 = (s32[16]{0:T(128)S(1)}, s32[16]{0:T(128)}, u32[]{:S(2)}) copy-start(s32[16]{0:T(128)} %param.12) | copy-start | bytes 196
  0.0 18.3 %copy-start = (bf16[16,14,8,64]{3,2,1,0:T(8,128)(2,1)S(1)}, bf16[16,14,8,64]{3,2,1,0:T(8,128)(2,1)}, u32[]{:S(2)}) copy-start(bf16[16,14,8,64]{3,2,1,0:T(8,128)(2,1)} %hop.1) | copy-start | bytes 688132
  0.0 34.5 %copy-start.3 = (s32[16,14]{1,0:T(8,128)S(1)}, s32[16,14]{1,0:T(8,128)}, u32[]{:S(2)}) copy-start(s32[16,14]{1,0:T(8,128)} %off.1) | copy-start | bytes 2692
  1.9 32.6 %collective-permute-start.1 = (s16[1040,256]{1,0:T(8,128)(2,1)S(1)}, s16[1040,256]{1,0:T(8,128)(2,1)S(1)}, u32[]{:S(2)}, u32[]{:S(2)}) collective-permute-start(s16[1040,256]{1,0:T(8,128)(2,1)S(1)} %get-tuple-element.11), channel_id=1, source_target_pairs={{0,8},{8,16},{16,24},{24,32},{32,40},{40,48},{48,56},{56,64},{64,7... | collective-permute-start | bytes 1597448 | tf_op jit(solution)/shard_map/ppermute | solution.py:177
  6.0 28.6 %collective-permute-start = (s16[1040,256]{1,0:T(8,128)(2,1)S(1)}, s16[1040,256]{1,0:T(8,128)(2,1)S(1)}, u32[]{:S(2)}, u32[]{:S(2)}) collective-permute-start(s16[1040,256]{1,0:T(8,128)(2,1)S(1)} %get-tuple-element.11), channel_id=1, source_target_pairs={{8,0},{16,8},{24,16},{32,24},{40,32},{48,40},{56,48},{64,56},{72,6... | collective-permute-start | bytes 1597448 | tf_op jit(solution)/shard_map/ppermute | solution.py:178

commit v5 on v4

--- a/solution.py
+++ b/solution.py
@@ -83,7 +83,7 @@
     pay[orbs:] = jnp.concatenate(codes, axis=0).astype(I32).astype(I16)
 
 
-def slots_kernel(hop_ref, own_ref, next_ref, prev_ref, phase, off, out, xs, tiles_v, out_v, phase_s, off_s, sems, out_sems):
+def slots_kernel(hop_ref, own_ref, prev_ref, next_ref, phase, off, out, xs, tiles_v, out_v, phase_s, off_s, sems, out_sems):
     peers, blocks, group, depth = hop_ref.shape
     rows = peers * group
     slots = off.shape[1]
@@ -120,16 +120,15 @@
     for pair in range(blocks // 2):
         res = []
         for i in (2 * pair, 2 * pair + 1):
-            a = jnp.zeros((rows, 2 * states), F32)
-            b = jnp.zeros((rows, 2 * states), F32)
             for s in range(slots):
                 prod = jnp.dot(
                     tiles_v[i, s] if i < early else left(i, s),
                     xs[off_s[i, s] + (i + blocks)],
                     preferred_element_type=F32,
                 )
-                a = a + phase_s[i, s] * prod
-                b = b + phase_s[blocks + i, s] * prod
+                cos_term = phase_s[i, s] * prod
+                sin_term = phase_s[blocks + i, s] * prod
+                a, b = (cos_term, sin_term) if s == 0 else (a + cos_term, b + sin_term)
             res.append((a[:, states:] + b[:, :states], b[:, states:] - a[:, :states]))
         cols = pl.ds(pair * 2 * rows, 2 * rows)
         out_v[0, :, cols] = jnp.concatenate([res[0][0], res[1][0]], axis=0).T
@@ -193,7 +192,7 @@
         ],
         compiler_params=pltpu.CompilerParams(vmem_limit_bytes=40 * 1024 * 1024),
         name="slots",
-    )(tiles, own, after, before, phase, offsets)
+    )(tiles, own, before, after, phase, offsets)
 
 
 def solution(mesh):

time: 39.6 us -> 39.6 us (level)
    ppermute x1, starting transfers between devices: 12.3 us -> 14.4 us  [on_device(): after = lax.ppermute(payload, 'orb', down)]
    ppermute x1, starting transfers between devices: 4.03 us -> 1.92 us  [on_device(): before = lax.ppermute(payload, 'orb', up)]
where the time goes in v5:
time: 39.6 us; the launch traced here: 39.5 us
  starting transfers between devices  16.3 us (41%)
  blocking collectives  15.9 us (40%)
  Pallas kernels  7.08 us (18%)
    all_gather x1, blocking collectives, on_device(): tiles = lax.all_gather(part, 'st')  15.9 us
    ppermute x1, starting transfers between devices, on_device(): after = lax.ppermute(payload, 'orb', down)  14.4 us
    pallas_call x1, Pallas kernels, on_device(): pl.pallas_call(slots_kernel, out_shape=jax.ShapeDtypeStruct((2, states, o...  4.82 us
    ppermute x1, starting transfers between devices, on_device(): before = lax.ppermute(payload, 'orb', up)  1.92 us
    pallas_call x1, Pallas kernels, on_device(): pl.pallas_call(functools.partial(segment_kernel, width), out_shape=(jax.S...  1.88 us
  transfers between devices with their start and end apart: 2, of which 0 were waited for; matrix products, arithmetic and copies ran while one was open for 0% of the time, Pallas kernels for 1%

profile of v5, /device:TPU:1, one launch (start us, length us, event | category | flops | bytes accessed | tf_op | source)
XLA Modules:
  0.0 39.5 jit_solution(6562748529838134402)
XLA Ops:
  0.0 0.0 copy-start.5
  0.0 0.0 copy-start.2
  0.0 0.0 copy-start.1
  0.0 0.0 copy-start.4
  0.0 0.0 copy-start
  0.0 0.0 copy-start.3
  0.0 1.9 %segment.1 = (bf16[16,128,256]{2,1,0:T(8,128)(2,1)S(1)}, s16[1040,256]{1,0:T(8,128)(2,1)S(1)}) custom-call(f32[2,128,1024]{2,1,0:T(8,128)} %wave.1, f32[2,128,1024]{2,1,0:T(8,128)} %slope.1), custom_call_target="tpu_custom_call" | custom-call | tf_op jit(solution)/shard_map/segment/pallas_call | solution.py:150
  1.9 14.4 %collective-permute-start.1 = (s16[1040,256]{1,0:T(8,128)(2,1)S(1)}, s16[1040,256]{1,0:T(8,128)(2,1)S(1)}, u32[]{:S(2)}, u32[]{:S(2)}) collective-permute-start(s16[1040,256]{1,0:T(8,128)(2,1)S(1)} %get-tuple-element.11), channel_id=1, source_target_pairs={{8,0},{16,8},{24,16},{32,24},{40,32},{48,40},{56,48},{64,56},{72,6... | collective-permute-start | bytes 1597448 | tf_op jit(solution)/shard_map/ppermute | solution.py:177
  16.3 1.9 %collective-permute-start = (s16[1040,256]{1,0:T(8,128)(2,1)S(1)}, s16[1040,256]{1,0:T(8,128)(2,1)S(1)}, u32[]{:S(2)}, u32[]{:S(2)}) collective-permute-start(s16[1040,256]{1,0:T(8,128)(2,1)S(1)} %get-tuple-element.11), channel_id=1, source_target_pairs={{0,8},{8,16},{16,24},{24,32},{32,40},{40,48},{48,56},{56,64},{64,7... | collective-permute-start | bytes 1597448 | tf_op jit(solution)/shard_map/ppermute | solution.py:176
  18.3 0.0 copy-done.5
  18.3 0.0 copy-done.2
  18.3 0.0 copy-done.1
  18.3 0.0 copy-done.4
  18.3 0.0 copy-done
  18.3 0.4 tiles.1
  18.7 15.9 %all-gather.2 = s16[128,8,896]{2,1,0:T(8,128)(2,1)S(1)} all-gather(s16[16,8,896]{2,1,0:T(8,128)(2,1)S(1)} %get-tuple-element.9), channel_id=2, replica_groups=mesh['orb'=64,'st'=8] {'st'}, dimensions={0}, use_global_device_ids=true | all-gather | bytes 2064384 | tf_op jit(solution)/shard_map/all_gather | solution.py:178
  34.6 0.0 collective-permute-done.1.next_ref
  34.6 0.0 collective-permute-done.prev_ref
  34.6 0.0 copy-done.3
  34.6 4.8 %slots.1 = f32[2,128,1024]{2,1,0:T(8,128)} custom-call(s16[8,16,8,896]{3,2,1,0:T(8,128)(2,1)S(1)} %bitcast.3, bf16[16,128,256]{2,1,0:T(8,128)(2,1)S(1)} %get-tuple-element.10.own_ref, s16[1040,256]{1,0:T(8,128)(2,1)S(1)} %collective-permute-done.prev_ref, s16[1040,256]{1,0:T(8,128)(2,1)S(1)} %collective-permute-done.1.next_ref, ...), custom_call_target="tpu_custom_call" | custom-call | tf_op jit(solution)/shard_map/slots/pallas_call | solution.py:179
Async XLA Ops:
  0.0 18.3 %copy-start.5 = (f32[3]{0:T(128)S(1)}, f32[3]{0:T(128)}, u32[]{:S(2)}) copy-start(f32[3]{0:T(128)} %param.15) | copy-start | bytes 40
  0.0 18.3 %copy-start.2 = (s32[3,16,14]{2,1,0:T(8,128)S(1)}, s32[3,16,14]{2,1,0:T(8,128)}, u32[]{:S(2)}) copy-start(s32[3,16,14]{2,1,0:T(8,128)} %shift.1) | copy-start | bytes 8068
  0.0 18.3 %copy-start.1 = (f32[3,16,14]{2,1,0:T(8,128)S(1)}, f32[3,16,14]{2,1,0:T(8,128)}, u32[]{:S(2)}) copy-start(f32[3,16,14]{2,1,0:T(8,128)} %bond.1) | copy-start | bytes 8068
  0.0 18.3 %copy-start.4 = (s32[16]{0:T(128)S(1)}, s32[16]{0:T(128)}, u32[]{:S(2)}) copy-start(s32[16]{0:T(128)} %param.12) | copy-start | bytes 196
  0.0 18.3 %copy-start = (bf16[16,14,8,64]{3,2,1,0:T(8,128)(2,1)S(1)}, bf16[16,14,8,64]{3,2,1,0:T(8,128)(2,1)}, u32[]{:S(2)}) copy-start(bf16[16,14,8,64]{3,2,1,0:T(8,128)(2,1)} %hop.1) | copy-start | bytes 688132
  0.0 34.6 %copy-start.3 = (s32[16,14]{1,0:T(8,128)S(1)}, s32[16,14]{1,0:T(8,128)}, u32[]{:S(2)}) copy-start(s32[16,14]{1,0:T(8,128)} %off.1) | copy-start | bytes 2692
  1.9 32.7 %collective-permute-start.1 = (s16[1040,256]{1,0:T(8,128)(2,1)S(1)}, s16[1040,256]{1,0:T(8,128)(2,1)S(1)}, u32[]{:S(2)}, u32[]{:S(2)}) collective-permute-start(s16[1040,256]{1,0:T(8,128)(2,1)S(1)} %get-tuple-element.11), channel_id=1, source_target_pairs={{8,0},{16,8},{24,16},{32,24},{40,32},{48,40},{56,48},{64,56},{72,6... | collective-permute-start | bytes 1597448 | tf_op jit(solution)/shard_map/ppermute | solution.py:177
  16.3 18.3 %collective-permute-start = (s16[1040,256]{1,0:T(8,128)(2,1)S(1)}, s16[1040,256]{1,0:T(8,128)(2,1)S(1)}, u32[]{:S(2)}, u32[]{:S(2)}) collective-permute-start(s16[1040,256]{1,0:T(8,128)(2,1)S(1)} %get-tuple-element.11), channel_id=1, source_target_pairs={{0,8},{8,16},{16,24},{24,32},{32,40},{40,48},{48,56},{56,64},{64,7... | collective-permute-start | bytes 1597448 | tf_op jit(solution)/shard_map/ppermute | solution.py:176
